TPU v7x, 128 devices: a whole 4x4x4 slice. The times are simulated.
128 devices in a mesh: gx: 16 (over x, y), gy: 8 (over z, core).
Axes of the slice: x: 4, y: 4, z: 4, core: 2. Of those that a mesh axis runs over, the one named last changes fastest.
Arguments:
- volume: bfloat16 [26, 512, 4096], P(None, 'gx', 'gy'), may hold values from -6 to 6
- owner: int32 [16, 8, 32, 1], P('gx', 'gy'), may hold values from 0 to 127; in each aligned block of 32 rows (0 to 31, 32 to 63, ..., all dimensions but the last counted through in order) at most 2 rows name the same one
- flags: int32 [16, 8, 32], P('gx', 'gy'), may hold values 0 or 1
Outputs:
- geometry: float32 [7, 4, 128, 1024], P(None, None, 'gx', 'gy')
- received: float32 [128, 256, 7, 128], P(('gx', 'gy'))
Inputs may be any that keep to these rules, and one draw needn't show every extreme that they name: Within the rows of one device, at most 2 name the same owner, and in every draw some owner is named by exactly 2 rows of some device.
All inputs are finite; a program needn't handle non-finite values. No bound on the sum of `flags` on one device may be relied on, other than what follows from the above.
Results may differ from a plain program's by a relative error of at most 0.0003.
Values may be sent and summed in bfloat16 or wider, within the bound.
A program may use at most 128 MiB of HBM per device.

v0:
```python
import math

import jax
import jax.numpy as jnp
from jax import lax
from jax.sharding import PartitionSpec as P

raw_taps = [math.exp(-((offset - 4) ** 2) / 8.0) for offset in range(9)]
gauss_taps = [value / sum(raw_taps) for value in raw_taps]
sharpness = 20.0
normal_floor = 0.01


def with_halo(block, sides, width):
    for axis, dim in sides:
        count = lax.axis_size(axis)
        forward = [(i, i + 1) for i in range(count - 1)]
        backward = [(target, source) for source, target in forward]
        low = lax.ppermute(
            lax.slice_in_dim(block, block.shape[dim] - width, None, axis=dim), axis, forward
        )
        high = lax.ppermute(lax.slice_in_dim(block, 0, width, axis=dim), axis, backward)
        block = jnp.concatenate([low, block, high], axis=dim)
    return block


def smooth_valid(padded):
    planes = padded.shape[0] - 8
    along_z = gauss_taps[0] * padded[0:planes].astype(jnp.float32)
    for offset in range(1, 9):
        along_z = along_z + gauss_taps[offset] * padded[offset : offset + planes].astype(
            jnp.float32
        )
    width_x = padded.shape[1] - 8
    along_x = gauss_taps[0] * along_z[:, 0:width_x]
    for offset in range(1, 9):
        along_x = along_x + gauss_taps[offset] * along_z[:, offset : offset + width_x]
    width_y = padded.shape[2] - 8
    along_y = gauss_taps[0] * along_x[:, :, 0:width_y]
    for offset in range(1, 9):
        along_y = along_y + gauss_taps[offset] * along_x[:, :, offset : offset + width_y]
    return along_y


def pair_smooth(field, axis):
    length = field.shape[axis] - 2
    lower = lax.slice_in_dim(field, 0, length, axis=axis)
    middle = lax.slice_in_dim(field, 1, length + 1, axis=axis)
    upper = lax.slice_in_dim(field, 2, length + 2, axis=axis)
    return 0.25 * lower + 0.5 * middle + 0.25 * upper


def pair_slope(field, axis):
    length = field.shape[axis] - 2
    lower = lax.slice_in_dim(field, 0, length, axis=axis)
    upper = lax.slice_in_dim(field, 2, length + 2, axis=axis)
    return 0.5 * (upper - lower)


def features(indicator, layers):
    blur_z = pair_smooth(indicator, 0)
    slope_z = pair_slope(indicator, 0)
    grad_z = pair_smooth(pair_smooth(slope_z, 1), 2)
    grad_x = pair_smooth(pair_slope(blur_z, 1), 2)
    grad_y = pair_slope(pair_smooth(blur_z, 1), 2)
    inner = indicator[1:-1, 1:-1, 1:-1]
    cells_x = inner.shape[1] // 4
    cells_y = inner.shape[2] // 4

    def blocks(field):
        return field.reshape(layers, 4, cells_x, 4, cells_y, 4)

    inner_blocks = blocks(inner)
    fraction = jnp.mean(inner_blocks, axis=(1, 3, 5))
    aperture_z = jnp.mean(inner_blocks[:, 0], axis=(2, 4))
    aperture_x = jnp.mean(inner_blocks[:, :, :, 0], axis=(1, 4))
    aperture_y = jnp.mean(inner_blocks[..., 0], axis=(1, 3))
    mean_z = jnp.mean(blocks(grad_z), axis=(1, 3, 5))
    mean_x = jnp.mean(blocks(grad_x), axis=(1, 3, 5))
    mean_y = jnp.mean(blocks(grad_y), axis=(1, 3, 5))
    length = jnp.sqrt(mean_z * mean_z + mean_x * mean_x + mean_y * mean_y + normal_floor)
    return jnp.stack(
        [
            fraction,
            aperture_z,
            aperture_x,
            aperture_y,
            -mean_z / length,
            -mean_x / length,
            -mean_y / length,
        ]
    )


def body(volume, owner, flags):
    tile_x = volume.shape[1]
    tile_y = volume.shape[2]
    layers = (volume.shape[0] - 10) // 4
    count_x = lax.axis_size("gx")
    count_y = lax.axis_size("gy")
    padded = with_halo(volume, (("gx", 1), ("gy", 2)), 5)
    smooth = smooth_valid(padded)
    place_x = lax.axis_index("gx") * tile_x - 1 + jnp.arange(tile_x + 2, dtype=jnp.int32)
    place_y = lax.axis_index("gy") * tile_y - 1 + jnp.arange(tile_y + 2, dtype=jnp.int32)
    inside_x = (place_x >= 0) & (place_x < count_x * tile_x)
    inside_y = (place_y >= 0) & (place_y < count_y * tile_y)
    inside = inside_x[None, :, None] & inside_y[None, None, :]
    indicator = jnp.where(inside, jax.nn.sigmoid(sharpness * smooth), 0.0)
    geometry = features(indicator, layers)
    cells_y = geometry.shape[3]
    row_count = layers * geometry.shape[2]
    rows_out = jnp.transpose(geometry.reshape(7, row_count, cells_y), (1, 0, 2))
    owners_local = owner.reshape(row_count)
    flags_local = flags.reshape(row_count)
    device_count = count_x * count_y
    capacity = max(2, 2 * row_count // device_count)
    targets = jnp.arange(device_count, dtype=jnp.int32)
    chosen = ((owners_local[:, None] == targets[None, :]) & (flags_local[:, None] == 1)).astype(
        jnp.int32
    )
    before = jnp.cumsum(chosen, axis=0) - chosen
    slots = jnp.sum(before * chosen, axis=1)
    dump = device_count * capacity
    target = jnp.where(flags_local == 1, owners_local * capacity + slots, dump)
    buffer = jnp.zeros((dump + 1, 7, cells_y), jnp.float32).at[target].set(rows_out)
    outgoing = buffer[:-1].reshape(device_count, capacity, 7, cells_y)
    arrived = lax.all_to_all(outgoing, ("gx", "gy"), split_axis=0, concat_axis=0, tiled=True)
    received = arrived.reshape(1, device_count * capacity, 7, cells_y)
    return (geometry, received)


def solution(mesh):
    in_specs = (P(None, "gx", "gy"), P("gx", "gy", None, None), P("gx", "gy", None))
    out_specs = (P(None, None, "gx", "gy"), P(("gx", "gy"), None, None, None))
    return jax.shard_map(body, mesh=mesh, in_specs=in_specs, out_specs=out_specs, check_vma=False)
```

profile of v0, /device:TPU:1, one launch (start us, length us, event | category | flops | bytes accessed | tf_op | source)
XLA Modules:
  0.0 292.1 jit_solution(7794480852400814172)
XLA Ops:
  0.6 0.0 copy-start.3
  0.7 1.2 fusion.39
  1.8 4.0 %collective-permute-start = (bf16[26,5,512]{2,1,0:T(8,128)(2,1)S(1)}, bf16[26,5,512]{2,1,0:T(8,128)(2,1)S(1)}, u32[]{:S(2)}, u32[]{:S(2)}) collective-permute-start(bf16[26,5,512]{2,1,0:T(8,128)(2,1)S(1)} %get-tuple-element.14), channel_id=1, source_target_pairs={{0,8},{8,16},{16,24},{24,32},{32,40},{40,48},{48,56},{56,64},{64,7... | collective-permute-start | bytes 399368 | tf_op jit(solution)/shard_map/ppermute | solution.py:19
  5.9 1.3 collective-permute-start.1
  7.2 0.7 compare_bitcast_fusion
  7.9 0.1 broadcast_and_fusion
  8.0 0.7 fusion.34
  8.7 0.1 reduce_window_sum.11
  8.8 0.8 select_reduce_fusion
  9.6 0.2 collective-permute-done
  9.8 3.8 %collective-permute-done.1 = bf16[26,5,512]{2,1,0:T(8,128)(2,1)S(1)} collective-permute-done((bf16[26,5,512]{2,1,0:T(8,128)(2,1)S(1)}, bf16[26,5,512]{2,1,0:T(8,128)(2,1)S(1)}, u32[]{:S(2)}, u32[]{:S(2)}) %collective-permute-start.1) | collective-permute-done | bytes 133152 | tf_op jit(solution)/shard_map/ppermute | solution.py:22
  13.6 1.3 pad_maximum_fusion.3
  14.9 5.3 %collective-permute-start.2 = (bf16[26,42,5]{2,1,0:T(8,128)(2,1)S(1)}, bf16[26,42,5]{2,1,0:T(8,128)(2,1)S(1)}, u32[]{:S(2)}, u32[]{:S(2)}) collective-permute-start(bf16[26,42,5]{2,1,0:T(8,128)(2,1)S(1)} %get-tuple-element.12), channel_id=1, source_target_pairs={{0,1},{1,2},{2,3},{3,4},{4,5},{5,6},{6,7},{8,9},{9,10},{10,11},{11... | collective-permute-start | bytes 32768 | tf_op jit(solution)/shard_map/ppermute | solution.py:19
  20.2 1.9 collective-permute-start.3
  22.2 1.9 collective-permute-done.2
  24.1 4.4 %collective-permute-done.3 = bf16[26,42,5]{2,1,0:T(8,128)(2,1)S(1)} collective-permute-done((bf16[26,42,5]{2,1,0:T(8,128)(2,1)S(1)}, bf16[26,42,5]{2,1,0:T(8,128)(2,1)S(1)}, u32[]{:S(2)}, u32[]{:S(2)}) %collective-permute-start.3) | collective-permute-done | bytes 10952 | tf_op jit(solution)/shard_map/ppermute | solution.py:22
  28.5 1.7 pad_maximum_fusion
  30.2 2.1 multiply_add_fusion
  32.3 1.9 fusion.13
  34.2 4.0 %fusion.21 = f32[18,34,514]{2,1,0:T(8,128)S(1)} fusion(f32[18,34,522]{2,1,0:T(8,128)S(1)} %fusion.13, pred[34,514]{1,0:T(8,128)(4,1)S(1)} %broadcast_and_fusion), kind=kLoop, calls=%fused_computation.44 | loop fusion | flops 6920496 | bytes 12600196 | tf_op jit(solution)/shard_map/jit(_where)/select_n | solution.py:108
  38.3 0.4 slice.243
  38.6 35.9 %reshape.418 = f32[4,4,8,4,128,4]{5,4,3,2,1,0:T(8,128)} reshape(f32[16,32,512]{2,1,0:T(8,128)S(1)} %slice.243) | data formatting | bytes 2097152 | tf_op jit(solution)/shard_map/reshape | solution.py:71
  74.6 4.0 %slice_reduce_fusion.2 = f32[4,8,128]{2,1,0:T(8,128)S(1)} fusion(f32[4,4,8,4,128,4]{5,4,3,2,1,0:T(8,128)} %reshape.418), kind=kLoop, calls=%fused_computation.3 | loop fusion | flops 61440 | bytes 278528 | tf_op jit(solution)/shard_map/reduce_sum | solution.py:75
  78.6 4.0 %slice_reduce_fusion.1 = f32[4,8,128]{2,1,0:T(8,128)S(1)} fusion(f32[4,4,8,4,128,4]{5,4,3,2,1,0:T(8,128)} %reshape.418), kind=kLoop, calls=%fused_computation.2 | loop fusion | flops 61440 | bytes 278528 | tf_op jit(solution)/shard_map/reduce_sum | solution.py:76
  82.6 12.2 %slice_reduce_fusion = f32[4,8,128]{2,1,0:T(8,128)S(1)} fusion(f32[4,4,8,4,128,4]{5,4,3,2,1,0:T(8,128)} %reshape.418), kind=kLoop, calls=%fused_computation.1 | loop fusion | flops 61440 | bytes 278528 | tf_op jit(solution)/shard_map/reduce_sum | solution.py:77
  94.9 1.5 subtract_multiply_fusion
  96.3 12.3 %reduce_sum.74 = f32[4,8,128]{2,1,0:T(8,128)S(1)} reduce(f32[4,4,8,4,128,4]{5,4,3,2,1,0:T(8,128)} %reshape.418, f32[]{:T(128)} %constant.40.clone.1), dimensions={1,3,5}, to_apply=%region_0.1 | reduce | flops 258048 | bytes 1064964 | tf_op jit(solution)/shard_map/reduce_sum | solution.py:74
  108.7 0.6 broadcast_multiply_fusion.2
  109.4 2.3 subtract_multiply_fusion.1
  111.7 0.6 fusion.31
  112.3 36.0 %reshape.419 = f32[4,4,8,4,128,4]{5,4,3,2,1,0:T(8,128)} reshape(f32[16,32,512]{2,1,0:T(8,128)S(1)} %fusion.31) | data formatting | bytes 2097152 | tf_op jit(solution)/shard_map/reshape | solution.py:71
  148.2 12.3 %reduce_sum.78 = f32[4,8,128]{2,1,0:T(8,128)S(1)} reduce(f32[4,4,8,4,128,4]{5,4,3,2,1,0:T(8,128)} %reshape.419, f32[]{:T(128)} %constant.40.clone.1), dimensions={1,3,5}, to_apply=%region_4.5 | reduce | flops 258048 | bytes 1064964 | tf_op jit(solution)/shard_map/reduce_sum | solution.py:78
  160.6 0.6 fusion.29
  161.2 36.2 %reshape.420 = f32[4,4,8,4,128,4]{5,4,3,2,1,0:T(8,128)} reshape(f32[16,32,512]{2,1,0:T(8,128)S(1)} %fusion.29) | data formatting | bytes 2097152 | tf_op jit(solution)/shard_map/reshape | solution.py:71
  197.4 12.3 %reduce_sum.79 = f32[4,8,128]{2,1,0:T(8,128)S(1)} reduce(f32[4,4,8,4,128,4]{5,4,3,2,1,0:T(8,128)} %reshape.420, f32[]{:T(128)} %constant.40.clone.1), dimensions={1,3,5}, to_apply=%region_5.6 | reduce | flops 258048 | bytes 1064964 | tf_op jit(solution)/shard_map/reduce_sum | solution.py:79
  209.7 0.3 fusion.28
  210.0 36.0 %reshape.421 = f32[4,4,8,4,128,4]{5,4,3,2,1,0:T(8,128)} reshape(f32[16,32,512]{2,1,0:T(8,128)S(1)} %fusion.28) | data formatting | bytes 2097152 | tf_op jit(solution)/shard_map/reshape | solution.py:71
  246.0 12.2 %reduce_sum.80 = f32[4,8,128]{2,1,0:T(8,128)S(1)} reduce(f32[4,4,8,4,128,4]{5,4,3,2,1,0:T(8,128)} %reshape.421, f32[]{:T(128)} %constant.40.clone.1), dimensions={1,3,5}, to_apply=%region_6.7 | reduce | flops 258048 | bytes 1064964 | tf_op jit(solution)/shard_map/reduce_sum | solution.py:80
  258.2 0.6 constant_dynamic-update-slice_fusion.2
  258.8 0.6 constant_dynamic-update-slice_fusion.1
  259.4 0.6 constant_dynamic-update-slice_fusion
  260.1 0.2 stack.5
  260.2 0.1 broadcast_in_dim.25
  260.3 1.5 scatter_fusion
  261.8 0.1 slice.264
  261.9 0.5 copy.36
  262.4 28.5 %all_to_all.5 = f32[128,2,7,128]{3,1,2,0:T(2,128)S(1)} all-to-all(f32[128,2,7,128]{3,1,2,0:T(2,128)S(1)} %copy.36), channel_id=1, replica_groups=mesh['gx'=16,'gy'=8] {'gx','gy'}, dimensions={0} | all-to-all | bytes 1835008 | tf_op jit(solution)/shard_map/all_to_all | solution.py:127
  290.9 1.2 copy.37
  (25 shorter events, 0.1 us)
Async XLA Ops:
  0.6 27.9 %copy-start.3 = (bf16[26,32,512]{2,1,0:T(8,128)(2,1)S(1)}, bf16[26,32,512]{2,1,0:T(8,128)(2,1)}, u32[]{:S(2)}) copy-start(bf16[26,32,512]{2,1,0:T(8,128)(2,1)} %param.3) | copy-start | bytes 2555908
  0.6 21.5 %copy-start.7 = (s32[1,1,32]{2,1,0:T(1,128)S(1)}, s32[1,1,32]{2,1,0:T(1,128)}, u32[]{:S(2)}) copy-start(s32[1,1,32]{2,1,0:T(1,128)} %param.5) | copy-start | bytes 388
  0.7 21.5 %copy-start.5 = (s32[1,1,32,1]{2,3,1,0:T(1,128)S(1)}, s32[1,1,32,1]{2,3,1,0:T(1,128)}, u32[]{:S(2)}) copy-start(s32[1,1,32,1]{2,3,1,0:T(1,128)} %param.4) | copy-start | bytes 388
  1.8 7.9 %collective-permute-start = (bf16[26,5,512]{2,1,0:T(8,128)(2,1)S(1)}, bf16[26,5,512]{2,1,0:T(8,128)(2,1)S(1)}, u32[]{:S(2)}, u32[]{:S(2)}) collective-permute-start(bf16[26,5,512]{2,1,0:T(8,128)(2,1)S(1)} %get-tuple-element.14), channel_id=1, source_target_pairs={{0,8},{8,16},{16,24},{24,32},{32,40},{40,48},{48,56},{56,64},{64,7... | collective-permute-start | bytes 399368 | tf_op jit(solution)/shard_map/ppermute | solution.py:19
  5.9 7.7 %collective-permute-start.1 = (bf16[26,5,512]{2,1,0:T(8,128)(2,1)S(1)}, bf16[26,5,512]{2,1,0:T(8,128)(2,1)S(1)}, u32[]{:S(2)}, u32[]{:S(2)}) collective-permute-start(bf16[26,5,512]{2,1,0:T(8,128)(2,1)S(1)} %get-tuple-element.15), channel_id=1, source_target_pairs={{8,0},{16,8},{24,16},{32,24},{40,32},{48,40},{56,48},{64,56},{72,6... | collective-permute-start | bytes 399368 | tf_op jit(solution)/shard_map/ppermute | solution.py:22
  14.9 9.2 %collective-permute-start.2 = (bf16[26,42,5]{2,1,0:T(8,128)(2,1)S(1)}, bf16[26,42,5]{2,1,0:T(8,128)(2,1)S(1)}, u32[]{:S(2)}, u32[]{:S(2)}) collective-permute-start(bf16[26,42,5]{2,1,0:T(8,128)(2,1)S(1)} %get-tuple-element.12), channel_id=1, source_target_pairs={{0,1},{1,2},{2,3},{3,4},{4,5},{5,6},{6,7},{8,9},{9,10},{10,11},{11... | collective-permute-start | bytes 32768 | tf_op jit(solution)/shard_map/ppermute | solution.py:19
  20.2 8.3 %collective-permute-start.3 = (bf16[26,42,5]{2,1,0:T(8,128)(2,1)S(1)}, bf16[26,42,5]{2,1,0:T(8,128)(2,1)S(1)}, u32[]{:S(2)}, u32[]{:S(2)}) collective-permute-start(bf16[26,42,5]{2,1,0:T(8,128)(2,1)S(1)} %get-tuple-element.13), channel_id=1, source_target_pairs={{1,0},{2,1},{3,2},{4,3},{5,4},{6,5},{7,6},{9,8},{10,9},{11,10},{12... | collective-permute-start | bytes 32768 | tf_op jit(solution)/shard_map/ppermute | solution.py:22
  96.3 13.0 %copy-start = (f32[16,34,514]{2,1,0:T(8,128)S(1)}, f32[16,34,514]{2,1,0:T(8,128)}, u32[]{:S(2)}) copy-start(f32[16,34,514]{2,1,0:T(8,128)} %get-tuple-element.9) | copy-start | bytes 3355396
  109.3 2.3 copy-start.6
  148.2 12.3 %copy-start.1 = (f32[16,32,514]{2,1,0:T(8,128)S(1)}, f32[16,32,514]{2,1,0:T(8,128)}, u32[]{:S(2)}) copy-start(f32[16,32,514]{2,1,0:T(8,128)} %get-tuple-element.10) | copy-start | bytes 3158020
  197.3 12.3 %copy-start.2 = (f32[16,32,514]{2,1,0:T(8,128)S(1)}, f32[16,32,514]{2,1,0:T(8,128)}, u32[]{:S(2)}) copy-start(f32[16,32,514]{2,1,0:T(8,128)} %get-tuple-element.11) | copy-start | bytes 3158020
  246.0 14.1 %copy-start.4 = (f32[4,8,128]{2,1,0:T(8,128)S(1)}, f32[4,8,128]{2,1,0:T(8,128)}, u32[]{:S(2)}) copy-start(f32[4,8,128]{2,1,0:T(8,128)} %broadcast_multiply_fusion.2) | copy-start | bytes 49156
where the time goes:
time: 293 us; the launch traced here: 292 us
  local copies, waits for them, and re-layouts  149 us (51%)
  other arithmetic  90.7 us (31%)
  blocking collectives  28.5 us (10%)
  starting transfers between devices  12.6 us (4%)
  waiting for transfers between devices  10.3 us (4%)
    reshape x4, local copies, waits for them, and re-layouts, blocks(): return field.reshape(layers, 4, cells_x, 4, cells_y, 4)  144 us
    all_to_all x1, blocking collectives, body(): lax.all_to_all(outgoing, ('gx', 'gy'), split_axis=0, concat_axis=0, tiled...  28.5 us
    reduce_sum x1, other arithmetic, features(): fraction = jnp.mean(inner_blocks, axis=(1, 3, 5))  12.3 us
    reduce_sum x1, other arithmetic, features(): mean_z = jnp.mean(blocks(grad_z), axis=(1, 3, 5))  12.3 us
    reduce_sum x1, other arithmetic, features(): mean_x = jnp.mean(blocks(grad_x), axis=(1, 3, 5))  12.3 us
    reduce_sum x1, other arithmetic, features(): aperture_y = jnp.mean(inner_blocks[..., 0], axis=(1, 3))  12.2 us
    reduce_sum x1, other arithmetic, features(): mean_y = jnp.mean(blocks(grad_y), axis=(1, 3, 5))  12.2 us
    ppermute x2, starting transfers between devices, with_halo(): lax.ppermute(lax.slice_in_dim(block, block.shape[dim] - width, None, axis...  9.34 us
  transfers between devices with their start and end apart: 4, of which 4 were waited for; matrix products, arithmetic and copies ran while one was open for 1% of the time, Pallas kernels for 0%

commit v1 on v0

--- a/solution.py
+++ b/solution.py
@@ -1,8 +1,11 @@
+import functools
 import math
 
 import jax
 import jax.numpy as jnp
 from jax import lax
+from jax.experimental import pallas as pl
+from jax.experimental.pallas import tpu as pltpu
 from jax.sharding import PartitionSpec as P
 
 raw_taps = [math.exp(-((offset - 4) ** 2) / 8.0) for offset in range(9)]
@@ -92,6 +95,66 @@
     )
 
 
+def exchange_kernel(count_x, count_y, src_ref, dst_ref, own_sem, send_sem, recv_sem):
+    count = count_x * count_y
+    me = lax.axis_index("gx") * count_y + lax.axis_index("gy")
+    barrier = pltpu.get_barrier_semaphore()
+
+    def place(step):
+        other = lax.rem(me + step, count)
+        return other, (other // count_y, lax.rem(other, count_y))
+
+    def greet(step, carry):
+        pl.semaphore_signal(
+            barrier, inc=1, device_id=place(step)[1], device_id_type=pl.DeviceIdType.MESH
+        )
+        return carry
+
+    lax.fori_loop(1, count, greet, 0)
+    pl.semaphore_wait(barrier, count - 1)
+
+    def send(step, carry):
+        other, device = place(step)
+        pltpu.make_async_remote_copy(
+            src_ref=src_ref.at[other],
+            dst_ref=dst_ref.at[me],
+            send_sem=send_sem,
+            recv_sem=recv_sem,
+            device_id=device,
+            device_id_type=pl.DeviceIdType.MESH,
+        ).start()
+        return carry
+
+    lax.fori_loop(1, count, send, 0)
+    own = pltpu.make_async_copy(src_ref.at[me], dst_ref.at[me], own_sem)
+    own.start()
+    own.wait()
+    most = pl.ds(0, count - 1)
+    every = pltpu.make_async_remote_copy(
+        src_ref=src_ref.at[most],
+        dst_ref=dst_ref.at[most],
+        send_sem=send_sem,
+        recv_sem=recv_sem,
+        device_id=place(1)[1],
+        device_id_type=pl.DeviceIdType.MESH,
+    )
+    every.wait_send()
+    every.wait_recv()
+
+
+def exchange(outgoing, count_x, count_y):
+    return pl.pallas_call(
+        functools.partial(exchange_kernel, count_x, count_y),
+        out_shape=jax.ShapeDtypeStruct(outgoing.shape, outgoing.dtype),
+        in_specs=[pl.BlockSpec(memory_space=pltpu.VMEM)],
+        out_specs=pl.BlockSpec(memory_space=pltpu.VMEM),
+        scratch_shapes=[pltpu.SemaphoreType.DMA] * 3,
+        compiler_params=pltpu.CompilerParams(
+            collective_id=0, has_side_effects=True, vmem_limit_bytes=16 * 2**20
+        ),
+    )(outgoing)
+
+
 def body(volume, owner, flags):
     tile_x = volume.shape[1]
     tile_y = volume.shape[2]
@@ -124,7 +187,8 @@
     target = jnp.where(flags_local == 1, owners_local * capacity + slots, dump)
     buffer = jnp.zeros((dump + 1, 7, cells_y), jnp.float32).at[target].set(rows_out)
     outgoing = buffer[:-1].reshape(device_count, capacity, 7, cells_y)
-    arrived = lax.all_to_all(outgoing, ("gx", "gy"), split_axis=0, concat_axis=0, tiled=True)
+    outgoing = outgoing.reshape(device_count, capacity * 7, cells_y)
+    arrived = exchange(outgoing, count_x, count_y)
     received = arrived.reshape(1, device_count * capacity, 7, cells_y)
     return (geometry, received)
 

time: 293 us -> 289 us (0.986)
  blocking collectives: 28.5 us -> 0 us
  Pallas kernels: 0 us -> 23 us
    all_to_all x1 -> x0, blocking collectives: 28.5 us -> none  [body(): lax.all_to_all(outgoing, ('gx', 'gy'), split_axis=0, concat_axis=0, tiled...]
    pallas_call x0 -> x1, Pallas kernels: none -> 23 us  [exchange(): pl.pallas_call(functools.partial(exchange_kernel, count_x, count_y), out_...]
where the time goes in v1:
time: 289 us; the launch traced here: 286 us
  local copies, waits for them, and re-layouts  149 us (52%)
  other arithmetic  90.7 us (31%)
  Pallas kernels  23 us (8%)
  starting transfers between devices  12.6 us (4%)
  waiting for transfers between devices  10.3 us (4%)
    reshape x4, local copies, waits for them, and re-layouts, blocks(): return field.reshape(layers, 4, cells_x, 4, cells_y, 4)  144 us
    pallas_call x1, Pallas kernels, exchange(): pl.pallas_call(functools.partial(exchange_kernel, count_x, count_y), out_...  23 us
    reduce_sum x1, other arithmetic, features(): fraction = jnp.mean(inner_blocks, axis=(1, 3, 5))  12.3 us
    reduce_sum x1, other arithmetic, features(): mean_z = jnp.mean(blocks(grad_z), axis=(1, 3, 5))  12.3 us
    reduce_sum x1, other arithmetic, features(): mean_x = jnp.mean(blocks(grad_x), axis=(1, 3, 5))  12.3 us
    reduce_sum x1, other arithmetic, features(): aperture_y = jnp.mean(inner_blocks[..., 0], axis=(1, 3))  12.2 us
    reduce_sum x1, other arithmetic, features(): mean_y = jnp.mean(blocks(grad_y), axis=(1, 3, 5))  12.2 us
    ppermute x2, starting transfers between devices, with_halo(): lax.ppermute(lax.slice_in_dim(block, block.shape[dim] - width, None, axis...  9.34 us
  transfers between devices with their start and end apart: 4, of which 4 were waited for; matrix products, arithmetic and copies ran while one was open for 1% of the time, Pallas kernels for 0%

profile of v1, /device:TPU:1, one launch (start us, length us, event | category | flops | bytes accessed | tf_op | source)
XLA Modules:
  0.0 286.2 jit_solution(11165152897076649567)
XLA Ops:
  0.7 1.2 fusion.39
  1.8 4.0 %collective-permute-start = (bf16[26,5,512]{2,1,0:T(8,128)(2,1)S(1)}, bf16[26,5,512]{2,1,0:T(8,128)(2,1)S(1)}, u32[]{:S(2)}, u32[]{:S(2)}) collective-permute-start(bf16[26,5,512]{2,1,0:T(8,128)(2,1)S(1)} %get-tuple-element.18), channel_id=1, source_target_pairs={{0,8},{8,16},{16,24},{24,32},{32,40},{40,48},{48,56},{56,64},{64,7... | collective-permute-start | bytes 399368 | tf_op jit(solution)/shard_map/ppermute | solution.py:22
  5.9 1.3 collective-permute-start.1
  7.2 0.7 compare_bitcast_fusion
  7.9 0.1 broadcast_and_fusion
  8.0 0.7 fusion.34
  8.7 0.1 reduce_window_sum.11
  8.8 0.8 select_reduce_fusion
  9.6 0.2 collective-permute-done
  9.8 3.8 %collective-permute-done.1 = bf16[26,5,512]{2,1,0:T(8,128)(2,1)S(1)} collective-permute-done((bf16[26,5,512]{2,1,0:T(8,128)(2,1)S(1)}, bf16[26,5,512]{2,1,0:T(8,128)(2,1)S(1)}, u32[]{:S(2)}, u32[]{:S(2)}) %collective-permute-start.1) | collective-permute-done | bytes 133152 | tf_op jit(solution)/shard_map/ppermute | solution.py:25
  13.6 1.3 pad_maximum_fusion.3
  14.9 5.3 %collective-permute-start.2 = (bf16[26,42,5]{2,1,0:T(8,128)(2,1)S(1)}, bf16[26,42,5]{2,1,0:T(8,128)(2,1)S(1)}, u32[]{:S(2)}, u32[]{:S(2)}) collective-permute-start(bf16[26,42,5]{2,1,0:T(8,128)(2,1)S(1)} %get-tuple-element.16), channel_id=1, source_target_pairs={{0,1},{1,2},{2,3},{3,4},{4,5},{5,6},{6,7},{8,9},{9,10},{10,11},{11... | collective-permute-start | bytes 32768 | tf_op jit(solution)/shard_map/ppermute | solution.py:22
  20.2 1.9 collective-permute-start.3
  22.2 1.9 collective-permute-done.2
  24.1 4.4 %collective-permute-done.3 = bf16[26,42,5]{2,1,0:T(8,128)(2,1)S(1)} collective-permute-done((bf16[26,42,5]{2,1,0:T(8,128)(2,1)S(1)}, bf16[26,42,5]{2,1,0:T(8,128)(2,1)S(1)}, u32[]{:S(2)}, u32[]{:S(2)}) %collective-permute-start.3) | collective-permute-done | bytes 10952 | tf_op jit(solution)/shard_map/ppermute | solution.py:25
  28.5 1.7 pad_maximum_fusion
  30.2 2.1 multiply_add_fusion
  32.3 1.9 fusion.13
  34.2 4.0 %fusion.21 = f32[18,34,514]{2,1,0:T(8,128)S(1)} fusion(f32[18,34,522]{2,1,0:T(8,128)S(1)} %fusion.13, pred[34,514]{1,0:T(8,128)(4,1)S(1)} %broadcast_and_fusion), kind=kLoop, calls=%fused_computation.44 | loop fusion | flops 6920496 | bytes 12600196 | tf_op jit(solution)/shard_map/jit(_where)/select_n | solution.py:171
  38.3 0.4 slice.243
  38.6 35.9 %reshape.415 = f32[4,4,8,4,128,4]{5,4,3,2,1,0:T(8,128)} reshape(f32[16,32,512]{2,1,0:T(8,128)S(1)} %slice.243) | data formatting | bytes 2097152 | tf_op jit(solution)/shard_map/reshape | solution.py:74
  74.6 4.0 %slice_reduce_fusion.2 = f32[4,8,128]{2,1,0:T(8,128)S(1)} fusion(f32[4,4,8,4,128,4]{5,4,3,2,1,0:T(8,128)} %reshape.415), kind=kLoop, calls=%fused_computation.3 | loop fusion | flops 61440 | bytes 278528 | tf_op jit(solution)/shard_map/reduce_sum | solution.py:78
  78.6 4.0 %slice_reduce_fusion.1 = f32[4,8,128]{2,1,0:T(8,128)S(1)} fusion(f32[4,4,8,4,128,4]{5,4,3,2,1,0:T(8,128)} %reshape.415), kind=kLoop, calls=%fused_computation.2 | loop fusion | flops 61440 | bytes 278528 | tf_op jit(solution)/shard_map/reduce_sum | solution.py:79
  82.6 12.2 %slice_reduce_fusion = f32[4,8,128]{2,1,0:T(8,128)S(1)} fusion(f32[4,4,8,4,128,4]{5,4,3,2,1,0:T(8,128)} %reshape.415), kind=kLoop, calls=%fused_computation.1 | loop fusion | flops 61440 | bytes 278528 | tf_op jit(solution)/shard_map/reduce_sum | solution.py:80
  94.9 1.5 subtract_multiply_fusion
  96.3 12.3 %reduce_sum.74 = f32[4,8,128]{2,1,0:T(8,128)S(1)} reduce(f32[4,4,8,4,128,4]{5,4,3,2,1,0:T(8,128)} %reshape.415, f32[]{:T(128)} %constant.40.clone.1), dimensions={1,3,5}, to_apply=%region_0.1 | reduce | flops 258048 | bytes 1064964 | tf_op jit(solution)/shard_map/reduce_sum | solution.py:77
  108.7 0.6 broadcast_multiply_fusion.2
  109.4 2.3 subtract_multiply_fusion.1
  111.7 0.6 fusion.31
  112.3 36.0 %reshape.416 = f32[4,4,8,4,128,4]{5,4,3,2,1,0:T(8,128)} reshape(f32[16,32,512]{2,1,0:T(8,128)S(1)} %fusion.31) | data formatting | bytes 2097152 | tf_op jit(solution)/shard_map/reshape | solution.py:74
  148.2 12.3 %reduce_sum.78 = f32[4,8,128]{2,1,0:T(8,128)S(1)} reduce(f32[4,4,8,4,128,4]{5,4,3,2,1,0:T(8,128)} %reshape.416, f32[]{:T(128)} %constant.40.clone.1), dimensions={1,3,5}, to_apply=%region_4.5 | reduce | flops 258048 | bytes 1064964 | tf_op jit(solution)/shard_map/reduce_sum | solution.py:81
  160.6 0.6 fusion.29
  161.2 36.2 %reshape.417 = f32[4,4,8,4,128,4]{5,4,3,2,1,0:T(8,128)} reshape(f32[16,32,512]{2,1,0:T(8,128)S(1)} %fusion.29) | data formatting | bytes 2097152 | tf_op jit(solution)/shard_map/reshape | solution.py:74
  197.4 12.3 %reduce_sum.79 = f32[4,8,128]{2,1,0:T(8,128)S(1)} reduce(f32[4,4,8,4,128,4]{5,4,3,2,1,0:T(8,128)} %reshape.417, f32[]{:T(128)} %constant.40.clone.1), dimensions={1,3,5}, to_apply=%region_5.6 | reduce | flops 258048 | bytes 1064964 | tf_op jit(solution)/shard_map/reduce_sum | solution.py:82
  209.7 0.3 fusion.28
  210.0 36.0 %reshape.418 = f32[4,4,8,4,128,4]{5,4,3,2,1,0:T(8,128)} reshape(f32[16,32,512]{2,1,0:T(8,128)S(1)} %fusion.28) | data formatting | bytes 2097152 | tf_op jit(solution)/shard_map/reshape | solution.py:74
  246.0 12.2 %reduce_sum.80 = f32[4,8,128]{2,1,0:T(8,128)S(1)} reduce(f32[4,4,8,4,128,4]{5,4,3,2,1,0:T(8,128)} %reshape.418, f32[]{:T(128)} %constant.40.clone.1), dimensions={1,3,5}, to_apply=%region_6.7 | reduce | flops 258048 | bytes 1064964 | tf_op jit(solution)/shard_map/reduce_sum | solution.py:83
  258.2 0.6 constant_dynamic-update-slice_fusion.2
  258.8 0.6 constant_dynamic-update-slice_fusion.1
  259.4 0.6 constant_dynamic-update-slice_fusion
  260.1 0.2 stack.5
  260.2 0.1 broadcast_in_dim.25
  260.3 1.5 scatter_fusion
  261.8 0.1 slice.264
  261.9 0.1 reshape_reshape.3.src_ref
  262.0 23.0 %shard_map.50 = f32[128,14,128]{2,1,0:T(8,128)S(1)} custom-call(f32[128,14,128]{2,1,0:T(8,128)S(1)} %reshape_reshape.3.src_ref), custom_call_target="tpu_custom_call" | custom-call | tf_op jit(solution)/shard_map/pallas_call | solution.py:146
  285.0 0.1 reshape.419
  285.1 1.1 copy.20
  (26 shorter events, 0.1 us)
Async XLA Ops:
  0.6 27.9 %copy-start.3 = (bf16[26,32,512]{2,1,0:T(8,128)(2,1)S(1)}, bf16[26,32,512]{2,1,0:T(8,128)(2,1)}, u32[]{:S(2)}) copy-start(bf16[26,32,512]{2,1,0:T(8,128)(2,1)} %param.3) | copy-start | bytes 2555908
  0.6 21.5 %copy-start.7 = (s32[1,1,32]{2,1,0:T(1,128)S(1)}, s32[1,1,32]{2,1,0:T(1,128)}, u32[]{:S(2)}) copy-start(s32[1,1,32]{2,1,0:T(1,128)} %param.5) | copy-start | bytes 388
  0.7 21.5 %copy-start.5 = (s32[1,1,32,1]{2,3,1,0:T(1,128)S(1)}, s32[1,1,32,1]{2,3,1,0:T(1,128)}, u32[]{:S(2)}) copy-start(s32[1,1,32,1]{2,3,1,0:T(1,128)} %param.4) | copy-start | bytes 388
  1.8 7.9 %collective-permute-start = (bf16[26,5,512]{2,1,0:T(8,128)(2,1)S(1)}, bf16[26,5,512]{2,1,0:T(8,128)(2,1)S(1)}, u32[]{:S(2)}, u32[]{:S(2)}) collective-permute-start(bf16[26,5,512]{2,1,0:T(8,128)(2,1)S(1)} %get-tuple-element.18), channel_id=1, source_target_pairs={{0,8},{8,16},{16,24},{24,32},{32,40},{40,48},{48,56},{56,64},{64,7... | collective-permute-start | bytes 399368 | tf_op jit(solution)/shard_map/ppermute | solution.py:22
  5.9 7.7 %collective-permute-start.1 = (bf16[26,5,512]{2,1,0:T(8,128)(2,1)S(1)}, bf16[26,5,512]{2,1,0:T(8,128)(2,1)S(1)}, u32[]{:S(2)}, u32[]{:S(2)}) collective-permute-start(bf16[26,5,512]{2,1,0:T(8,128)(2,1)S(1)} %get-tuple-element.19), channel_id=1, source_target_pairs={{8,0},{16,8},{24,16},{32,24},{40,32},{48,40},{56,48},{64,56},{72,6... | collective-permute-start | bytes 399368 | tf_op jit(solution)/shard_map/ppermute | solution.py:25
  14.9 9.2 %collective-permute-start.2 = (bf16[26,42,5]{2,1,0:T(8,128)(2,1)S(1)}, bf16[26,42,5]{2,1,0:T(8,128)(2,1)S(1)}, u32[]{:S(2)}, u32[]{:S(2)}) collective-permute-start(bf16[26,42,5]{2,1,0:T(8,128)(2,1)S(1)} %get-tuple-element.16), channel_id=1, source_target_pairs={{0,1},{1,2},{2,3},{3,4},{4,5},{5,6},{6,7},{8,9},{9,10},{10,11},{11... | collective-permute-start | bytes 32768 | tf_op jit(solution)/shard_map/ppermute | solution.py:22
  20.2 8.3 %collective-permute-start.3 = (bf16[26,42,5]{2,1,0:T(8,128)(2,1)S(1)}, bf16[26,42,5]{2,1,0:T(8,128)(2,1)S(1)}, u32[]{:S(2)}, u32[]{:S(2)}) collective-permute-start(bf16[26,42,5]{2,1,0:T(8,128)(2,1)S(1)} %get-tuple-element.17), channel_id=1, source_target_pairs={{1,0},{2,1},{3,2},{4,3},{5,4},{6,5},{7,6},{9,8},{10,9},{11,10},{12... | collective-permute-start | bytes 32768 | tf_op jit(solution)/shard_map/ppermute | solution.py:25
  96.3 13.0 %copy-start = (f32[16,34,514]{2,1,0:T(8,128)S(1)}, f32[16,34,514]{2,1,0:T(8,128)}, u32[]{:S(2)}) copy-start(f32[16,34,514]{2,1,0:T(8,128)} %get-tuple-element.13) | copy-start | bytes 3355396
  109.3 2.3 copy-start.6
  148.2 12.3 %copy-start.1 = (f32[16,32,514]{2,1,0:T(8,128)S(1)}, f32[16,32,514]{2,1,0:T(8,128)}, u32[]{:S(2)}) copy-start(f32[16,32,514]{2,1,0:T(8,128)} %get-tuple-element.14) | copy-start | bytes 3158020
  197.3 12.3 %copy-start.2 = (f32[16,32,514]{2,1,0:T(8,128)S(1)}, f32[16,32,514]{2,1,0:T(8,128)}, u32[]{:S(2)}) copy-start(f32[16,32,514]{2,1,0:T(8,128)} %get-tuple-element.15) | copy-start | bytes 3158020
  246.0 14.1 %copy-start.4 = (f32[4,8,128]{2,1,0:T(8,128)S(1)}, f32[4,8,128]{2,1,0:T(8,128)}, u32[]{:S(2)}) copy-start(f32[4,8,128]{2,1,0:T(8,128)} %broadcast_multiply_fusion.2) | copy-start | bytes 49156

commit v2 on v0

v2 whole, which is shorter than its diff:
```python
import functools
import math

import jax
import jax.numpy as jnp
import ml_dtypes
import numpy as np
from jax import lax
from jax.experimental import pallas as pl
from jax.experimental.pallas import tpu as pltpu
from jax.sharding import PartitionSpec as P

MESH = pl.DeviceIdType.MESH

raw_taps = [math.exp(-((offset - 4) ** 2) / 8.0) for offset in range(9)]
gauss_taps = np.array([value / sum(raw_taps) for value in raw_taps])
sharpness = 20.0
normal_floor = 0.01

PLANES_IN = 26
TILE_X = 32
TILE_Y = 512
REACH = 5
GROUPS = 3
GROUP_PLANES = 6
WIDE_X = TILE_X + 2
GROUP_ROWS = 208
GROUP_IN = GROUP_PLANES + 8
SIDE_ROWS = 144
WINDOW = 96
WINDOW_AT = [(REACH * GROUP_PLANES * g) // 16 * 16 for g in range(GROUPS)]
ROWS = 32
CHANNELS = 7
LEVELS = 32766.0


def halves(matrix):
    high = matrix.astype(np.float32).astype(ml_dtypes.bfloat16)
    low = (matrix - high.astype(np.float64)).astype(np.float32).astype(ml_dtypes.bfloat16)
    return np.stack([high, low])


def pack_matrix():
    matrix = np.zeros((2 * SIDE_ROWS, PLANES_IN * TILE_X))
    for z in range(PLANES_IN):
        for i in range(REACH):
            matrix[z * REACH + i, z * TILE_X + i] = 1
            matrix[SIDE_ROWS + z * REACH + i, z * TILE_X + TILE_X - REACH + i] = 1
    return matrix.astype(ml_dtypes.bfloat16)


def tap(distance):
    return gauss_taps[distance + 4] if -4 <= distance <= 4 else 0.0


def own_matrix():
    matrix = np.zeros((GROUP_ROWS, GROUP_IN * TILE_X))
    for plane in range(GROUP_PLANES):
        for x in range(WIDE_X):
            for z in range(9):
                for source in range(TILE_X):
                    matrix[plane * WIDE_X + x, (plane + z) * TILE_X + source] = (
                        gauss_taps[z] * tap(source - (x - 1))
                    )
    return halves(matrix)


def side_matrices():
    found = []
    for g in range(GROUPS):
        matrix = np.zeros((GROUP_ROWS, 2 * WINDOW))
        for plane in range(GROUP_PLANES):
            for x in range(WIDE_X):
                for z in range(9):
                    for i in range(REACH):
                        row = (g * GROUP_PLANES + plane + z) * REACH + i - WINDOW_AT[g]
                        out = plane * WIDE_X + x
                        matrix[out, row] = gauss_taps[z] * tap(i - REACH - (x - 1))
                        matrix[out, WINDOW + row] = gauss_taps[z] * tap(TILE_X + i - (x - 1))
        found.append(halves(matrix))
    return np.stack(found)


def along_y_matrices():
    scale = -sharpness / math.log(2.0)
    main = np.zeros((512, 256))
    for out in range(256):
        for distance in range(-4, 5):
            main[128 + out + distance, out] = scale * tap(distance)
    edge = np.zeros((512, 128))
    for distance in range(-4, 5):
        edge[127 + distance, 0] = scale * tap(distance)
        edge[384 + distance, 1] = scale * tap(distance)
    return halves(main), halves(edge)


MEAN = np.array([0, 1, 1, 1, 1, 0]) / 4
FIRST = np.array([0, 1, 0, 0, 0, 0]) / 1
SOFT = np.array([1, 3, 4, 4, 3, 1]) / 16
SLOPE = np.array([-1, -1, 0, 0, 1, 1]) / 8


def cell_matrix():
    pairs = [(MEAN, MEAN), (FIRST, MEAN), (MEAN, FIRST), (SLOPE, SOFT), (SOFT, SLOPE), (SOFT, SOFT)]
    matrix = np.zeros((GROUPS, len(pairs) * ROWS, GROUP_ROWS))
    for at, (along_z, along_x) in enumerate(pairs):
        for layer in range(4):
            for cell in range(8):
                for z in range(6):
                    for x in range(6):
                        plane = 4 * layer + z
                        place = plane % GROUP_PLANES * WIDE_X + 4 * cell + x
                        matrix[plane // GROUP_PLANES, at * ROWS + layer * 8 + cell, place] += (
                            along_z[z] * along_x[x]
                        )
    return matrix.astype(ml_dtypes.bfloat16)


def cell_y_matrix():
    matrix = np.zeros((2, TILE_Y + 128, 256))
    for at, weights in enumerate((MEAN, FIRST, SOFT, SLOPE)):
        for cell in range(128):
            for y in range(6):
                place = 4 * cell + y - 1
                row = TILE_Y if place < 0 else TILE_Y + 1 if place >= TILE_Y else place
                matrix[at // 2, row, at % 2 * 128 + cell] = weights[y]
    return matrix.astype(ml_dtypes.bfloat16)


def side_marks():
    marks = np.zeros((8, GROUP_ROWS), np.float32)
    for plane in range(GROUP_PLANES):
        marks[0, plane * WIDE_X] = 1
        marks[1, plane * WIDE_X + WIDE_X - 1] = 1
    return marks


def split(value):
    high = value.astype(jnp.bfloat16)
    return high, (value - high.astype(jnp.float32)).astype(jnp.bfloat16)


def dot(left, right):
    return jnp.dot(left, right, preferred_element_type=jnp.float32)


def routing(owner, flags):
    wide = (ROWS, ROWS)
    row = lax.broadcasted_iota(jnp.int32, wide, 0)
    column = lax.broadcasted_iota(jnp.int32, wide, 1)
    owner_across = jnp.broadcast_to(owner.astype(jnp.float32), wide)
    flag_across = jnp.broadcast_to(flags.astype(jnp.float32), wide)
    same = row == column
    owner_down = jnp.sum(jnp.where(same, owner_across, 0.0), axis=1, keepdims=True)
    flag_down = jnp.sum(jnp.where(same, flag_across, 0.0), axis=1, keepdims=True)
    earlier = (column < row) & (owner_down == owner_across)
    slot = jnp.sum(jnp.where(earlier, flag_across, 0.0), axis=1, keepdims=True)
    code = jnp.where(flag_down > 0.5, owner_down * 2.0 + slot, -8.0)
    place = lax.broadcasted_iota(jnp.int32, (ROWS, 256), 1)
    mine = (place & (ROWS - 1)) == lax.broadcasted_iota(jnp.int32, (ROWS, 256), 0)
    spread = jnp.sum(jnp.where(mine, code, 0.0), axis=0, keepdims=True)
    part = ((lax.broadcasted_iota(jnp.int32, (1, 256), 1) >> 5) & 3).astype(jnp.float32)
    return spread * 4.0 + part


def kernel(
    count_x, count_y,
    volume, owner, flags, marks, pack_w, own_w, side_w, main_w, edge_w, cell_w, cell_y_w,
    geometry, arrived,
    tile, packed, sides, smooth, chosen, leaving,
    pack_v, own_v, side_v, main_v, edge_v, cell_v, cell_y_v,
    load_sem, send_sem, recv_sem, far_sem, out_send, out_recv,
):
    p = lax.axis_index("gx")
    q = lax.axis_index("gy")
    count = count_x * count_y
    me = p * count_y + q

    def at(dx, dy):
        return (lax.rem(p + dx + count_x, count_x), lax.rem(q + dy + count_y, count_y))

    around = [(dx, dy) for dx in (-1, 0, 1) for dy in (-1, 0, 1) if (dx, dy) != (0, 0)]
    barrier = pltpu.get_barrier_semaphore()
    loads = [
        pltpu.make_async_copy(source, target, load_sem.at[i])
        for i, (source, target) in enumerate(
            [
                (volume, tile.at[:, :, pl.ds(128, TILE_Y)]),
                (pack_w, pack_v),
                (own_w, own_v),
                (side_w, side_v),
                (main_w, main_v),
                (edge_w, edge_v),
                (cell_w, cell_v),
                (cell_y_w, cell_y_v),
            ]
        )
    ]
    for load in loads:
        load.start()
    for dx, dy in around:
        pl.semaphore_signal(barrier, inc=1, device_id=at(dx, dy), device_id_type=MESH)

    loads[0].wait()
    loads[1].wait()
    own = tile[:, :, 128:640].reshape(PLANES_IN * TILE_X, TILE_Y)
    packed[...] = dot(pack_v[...], own).astype(jnp.bfloat16)

    pl.semaphore_wait(barrier, len(around))
    for dx, dy in around:
        pl.semaphore_signal(far_sem.at[0], inc=1, device_id=at(dx, dy), device_id_type=MESH)
    sends = []
    for i, (dx, dy) in enumerate(around):
        there = pl.ds(640, 128) if dy < 0 else pl.ds(0, 128)
        if dx == 0:
            source = tile.at[:, :, pl.ds(128 if dy < 0 else 512, 128)]
            target = tile.at[:, :, there]
        else:
            rows = pl.ds(0 if dx < 0 else SIDE_ROWS, SIDE_ROWS)
            rows_there = pl.ds(SIDE_ROWS if dx < 0 else 0, SIDE_ROWS)
            if dy == 0:
                source = packed.at[rows, :]
                target = sides.at[rows_there, pl.ds(128, TILE_Y)]
            else:
                source = packed.at[rows, pl.ds(0 if dy < 0 else TILE_Y - 128, 128)]
                target = sides.at[rows_there, there]
        sends.append(
            pltpu.make_async_remote_copy(
                src_ref=source,
                dst_ref=target,
                send_sem=send_sem.at[i],
                recv_sem=recv_sem.at[i],
                device_id=at(dx, dy),
                device_id_type=MESH,
            )
        )
    for send in sends:
        send.start()

    loads[2].wait()
    for g in range(GROUPS):
        block = tile[g * GROUP_PLANES : g * GROUP_PLANES + GROUP_IN, :, 128:640].reshape(
            GROUP_IN * TILE_X, TILE_Y
        )
        smooth[g] = dot(own_v[0], block) + dot(own_v[1], block)

    codes = routing(owner[...], flags[...])
    number = lax.broadcasted_iota(jnp.int32, (count * 8, 256), 0).astype(jnp.float32)
    chosen[...] = jnp.where(number == codes, 1.0, 0.0).astype(jnp.bfloat16)

    pl.semaphore_wait(far_sem.at[0], len(around))
    for dx, dy in around:
        pl.semaphore_signal(
            far_sem.at[1], inc=1, device_id=at(2 * dx, 2 * dy), device_id_type=MESH
        )
    for load in loads[3:]:
        load.wait()
    for send in sends:
        send.wait()

    @pl.when(p == 0)
    def _():
        sides[0:SIDE_ROWS, :] = jnp.zeros((SIDE_ROWS, 768), jnp.bfloat16)

    @pl.when(p == count_x - 1)
    def _():
        sides[SIDE_ROWS : 2 * SIDE_ROWS, :] = jnp.zeros((SIDE_ROWS, 768), jnp.bfloat16)

    @pl.when(q == 0)
    def _():
        sides[:, 0:128] = jnp.zeros((2 * SIDE_ROWS, 128), jnp.bfloat16)
        tile[:, :, 0:128] = jnp.zeros((PLANES_IN, TILE_X, 128), jnp.bfloat16)

    @pl.when(q == count_y - 1)
    def _():
        sides[:, 640:768] = jnp.zeros((2 * SIDE_ROWS, 128), jnp.bfloat16)
        tile[:, :, 640:768] = jnp.zeros((PLANES_IN, TILE_X, 128), jnp.bfloat16)

    pl.semaphore_wait(far_sem.at[1], len(around))
    for dx in (-4, 4):
        pl.semaphore_signal(far_sem.at[2], inc=1, device_id=at(dx, 0), device_id_type=MESH)

    low_out = jnp.where(p == 0, 1.0, 0.0)
    high_out = jnp.where(p == count_x - 1, 1.0, 0.0)
    keep = (1.0 - low_out * marks[0:1, :] - high_out * marks[1:2, :]).astype(jnp.bfloat16)
    lane = lax.broadcasted_iota(jnp.int32, (1, 128), 1)
    left_out = jnp.where(q == 0, 0, -1)
    right_out = jnp.where(q == count_y - 1, 1, -1)
    edge_keep = jnp.where((lane == left_out) | (lane == right_out), 0.0, 1.0)

    def indicator(power):
        below = 1.0 + jnp.exp2(jnp.minimum(power, 126.0))
        guess = pl.reciprocal(below, approx=True)
        return guess * (2.0 - below * guess)

    cells = jnp.zeros((6 * ROWS, TILE_Y + 128), jnp.float32)
    for g in range(GROUPS):
        planes = slice(g * GROUP_PLANES, g * GROUP_PLANES + GROUP_IN)
        ends = jnp.concatenate([tile[planes, :, 0:128], tile[planes, :, 640:768]], axis=2).reshape(
            GROUP_IN * TILE_X, 256
        )
        first = WINDOW_AT[g]
        window = jnp.concatenate(
            [
                sides[first : first + WINDOW, :],
                sides[SIDE_ROWS + first : SIDE_ROWS + first + WINDOW, :],
            ],
            axis=0,
        )
        middle = (
            dot(side_v[g, 0], window[:, 128:640])
            + dot(side_v[g, 1], window[:, 128:640])
            + smooth[g]
        )
        beside = jnp.concatenate([window[:, 0:128], window[:, 640:768]], axis=1)
        outer = (
            dot(own_v[0], ends)
            + dot(own_v[1], ends)
            + dot(side_v[g, 0], beside)
            + dot(side_v[g, 1], beside)
        )
        high, low = split(
            jnp.concatenate([outer[:, 0:128], middle, outer[:, 128:256]], axis=1)
        )
        values = []
        for c in range(2):
            lanes = slice(256 * c, 256 * c + 512)
            values.append(
                indicator(
                    dot(high[:, lanes], main_v[0])
                    + dot(low[:, lanes], main_v[0])
                    + dot(high[:, lanes], main_v[1])
                )
            )
        high_edge = jnp.concatenate([high[:, 0:256], high[:, 512:768]], axis=1)
        low_edge = jnp.concatenate([low[:, 0:256], low[:, 512:768]], axis=1)
        values.append(
            edge_keep
            * indicator(
                dot(high_edge, edge_v[0]) + dot(low_edge, edge_v[0]) + dot(high_edge, edge_v[1])
            )
        )
        high, low = split(jnp.concatenate(values, axis=1))
        weights = cell_v[g] * keep
        cells = cells + dot(weights, high) + dot(weights, low)

    high, low = split(cells)
    plain = dot(high[0:96], cell_y_v[0]) + dot(low[0:96], cell_y_v[0])
    slopes = dot(high[96:192], cell_y_v[1]) + dot(low[96:192], cell_y_v[1])
    mean_z, mean_x, mean_y = slopes[0:32, 0:128], slopes[32:64, 0:128], slopes[64:96, 128:256]
    shrink = -lax.rsqrt(mean_z * mean_z + mean_x * mean_x + mean_y * mean_y + normal_floor)
    found = [
        plain[0:32, 0:128],
        plain[32:64, 0:128],
        plain[64:96, 0:128],
        plain[0:32, 128:256],
        mean_z * shrink,
        mean_x * shrink,
        mean_y * shrink,
    ]
    for channel in range(CHANNELS):
        geometry[channel] = found[channel]

    most = functools.reduce(jnp.maximum, [jnp.abs(value) for value in found])
    most = jnp.maximum(jnp.max(most, axis=1, keepdims=True), 1e-37)
    grade = jnp.ceil(8.0 * jnp.log2(most) + 0.02)
    stretch = jnp.exp2(grade * -0.125)
    whole = [jnp.floor(value * stretch * LEVELS + 0.5) for value in found]
    whole.append(jnp.broadcast_to(grade, (ROWS, 128)))
    coded = jnp.concatenate(
        [jnp.concatenate(whole[0:4], axis=0), jnp.concatenate(whole[4:8], axis=0)], axis=1
    )
    upper = jnp.floor(coded * (1.0 / 256.0) + 0.5) * 256.0
    stacked = jnp.concatenate([upper, coded - upper], axis=0).astype(jnp.bfloat16)
    placed = dot(chosen[...], stacked).astype(jnp.int32)
    joined = (placed[:, 128:256] << 16) | (placed[:, 0:128] & 0xFFFF)
    leaving[...] = joined.reshape(count, 8, 128)

    pl.semaphore_wait(far_sem.at[2], 2)

    def send_out(step, carry):
        other = lax.rem(me + step, count)
        pltpu.make_async_remote_copy(
            src_ref=leaving.at[other],
            dst_ref=arrived.at[me],
            send_sem=out_send,
            recv_sem=out_recv,
            device_id=(other // count_y, lax.rem(other, count_y)),
            device_id_type=MESH,
        ).start()
        return carry

    lax.fori_loop(1, count, send_out, 0)
    arrived[me] = leaving[me]
    others = pl.ds(0, count - 1)
    every = pltpu.make_async_remote_copy(
        src_ref=leaving.at[others],
        dst_ref=arrived.at[others],
        send_sem=out_send,
        recv_sem=out_recv,
        device_id=at(1, 0),
        device_id_type=MESH,
    )
    every.wait_send()
    every.wait_recv()


def decode_kernel(coded, geometry_in, received, geometry):
    geometry[...] = geometry_in[...]
    rows = received.shape[1]

    def pair(part):
        both = coded[pl.ds(part, rows, stride=4), :]
        return (both << 16) >> 16, both >> 16

    fourth, grade = pair(3)
    scale = jnp.exp2(grade.astype(jnp.float32) * 0.125) * (1.0 / LEVELS)
    received[3] = fourth.astype(jnp.float32) * scale
    for part in range(3):
        low, high = pair(part)
        received[part] = low.astype(jnp.float32) * scale
        received[part + 4] = high.astype(jnp.float32) * scale


def body(count_x, count_y, volume, owner, flags):
    count = count_x * count_y
    main_w, edge_w = along_y_matrices()
    weights = [
        pack_matrix(), own_matrix(), side_matrices(), main_w, edge_w, cell_matrix(), cell_y_matrix(),
    ]
    in_vmem = pl.BlockSpec(memory_space=pltpu.VMEM)
    anywhere = pl.BlockSpec(memory_space=pl.ANY)
    geometry, arrived = pl.pallas_call(
        functools.partial(kernel, count_x, count_y),
        out_shape=(
            jax.ShapeDtypeStruct((CHANNELS, ROWS, 128), jnp.float32),
            jax.ShapeDtypeStruct((count, 8, 128), jnp.int32),
        ),
        in_specs=[anywhere, in_vmem, in_vmem, in_vmem] + [anywhere] * len(weights),
        out_specs=(in_vmem, in_vmem),
        scratch_shapes=[
            pltpu.VMEM((PLANES_IN, TILE_X, 768), jnp.bfloat16),
            pltpu.VMEM((2 * SIDE_ROWS, TILE_Y), jnp.bfloat16),
            pltpu.VMEM((2 * SIDE_ROWS, 768), jnp.bfloat16),
            pltpu.VMEM((GROUPS, GROUP_ROWS, TILE_Y), jnp.float32),
            pltpu.VMEM((count * 8, 256), jnp.bfloat16),
            pltpu.VMEM((count, 8, 128), jnp.int32),
        ]
        + [pltpu.VMEM(weight.shape, jnp.bfloat16) for weight in weights]
        + [
            pltpu.SemaphoreType.DMA((1 + len(weights),)),
            pltpu.SemaphoreType.DMA((8,)),
            pltpu.SemaphoreType.DMA((8,)),
            pltpu.SemaphoreType.REGULAR((3,)),
            pltpu.SemaphoreType.DMA,
            pltpu.SemaphoreType.DMA,
        ],
        compiler_params=pltpu.CompilerParams(
            collective_id=0, has_side_effects=True, vmem_limit_bytes=62 * 2**20
        ),
    )(volume, owner.reshape(1, ROWS), flags.reshape(1, ROWS), side_marks(), *weights)
    received, geometry = pl.pallas_call(
        decode_kernel,
        out_shape=(
            jax.ShapeDtypeStruct((CHANNELS, count * 2, 128), jnp.float32),
            jax.ShapeDtypeStruct(geometry.shape, jnp.float32),
        ),
        in_specs=[in_vmem, in_vmem],
        out_specs=(in_vmem, in_vmem),
        compiler_params=pltpu.CompilerParams(vmem_limit_bytes=16 * 2**20),
    )(arrived.reshape(count * 8, 128), geometry)
    received = jnp.transpose(received, (1, 0, 2))[None]
    return (geometry.reshape(CHANNELS, 4, 8, 128), received)


def solution(mesh):
    in_specs = (P(None, "gx", "gy"), P("gx", "gy", None, None), P("gx", "gy", None))
    out_specs = (P(None, None, "gx", "gy"), P(("gx", "gy"), None, None, None))
    return jax.shard_map(
        functools.partial(body, mesh.shape["gx"], mesh.shape["gy"]),
        mesh=mesh,
        in_specs=in_specs,
        out_specs=out_specs,
        check_vma=False,
    )
```

time: 293 us -> 35.7 us (0.12)
  local copies, waits for them, and re-layouts: 149 us -> 1.93 us
  other arithmetic: 90.7 us -> 0 us
  Pallas kernels: 0 us -> 32.9 us
  blocking collectives: 28.5 us -> 0 us
  starting transfers between devices: 12.6 us -> 0 us
  waiting for transfers between devices: 10.3 us -> 0 us
    reshape x5 -> x0, local copies, waits for them, and re-layouts: 145 us -> none  [the longest x4 144 us: blocks(): return field.reshape(layers, 4, cells_x, 4, cells_y, 4)]
    reduce_sum x8 -> x0, other arithmetic: 70.2 us -> none  [the longest x1 12.3 us: features(): fraction = jnp.mean(inner_blocks, axis=(1, 3, 5))]
    pallas_call x0 -> x2, Pallas kernels: none -> 32.9 us  [the longest x1 31.8 us: body(): pl.pallas_call(functools.partial(kernel, count_x, count_y), out_shape=(ja...]
    all_to_all x1 -> x0, blocking collectives: 28.5 us -> none  [body(): lax.all_to_all(outgoing, ('gx', 'gy'), split_axis=0, concat_axis=0, tiled...]
    ppermute x4 -> x0, starting transfers between devices: 12.6 us -> none  [the longest x2 9.34 us: with_halo(): lax.ppermute(lax.slice_in_dim(block, block.shape[dim] - width, None, axis...]
    ppermute x4 -> x0, waiting for transfers between devices: 10.3 us -> none  [the longest x2 8.2 us: with_halo(): lax.ppermute(lax.slice_in_dim(block, 0, width, axis=dim), axis, backward)]
    add x4 -> x0, other arithmetic: 5.2 us -> none  [the longest x1 2.09 us: smooth_valid(): along_z + gauss_taps[offset] * padded[offset:offset + planes].astype(jnp....]
    mul x3 -> x0, other arithmetic: 4.14 us -> none  [pair_slope(): return 0.5 * (upper - lower)]
  transfers between devices with their start and end apart: 4 -> 0, of which waited for: 4 -> 0; matrix products, arithmetic and copies ran while one was open for 1% -> 0% of each run, Pallas kernels for 0% -> 0%
where the time goes in v2:
time: 35.7 us; the launch traced here: 35.5 us
  Pallas kernels  32.9 us (92%)
  local copies, waits for them, and re-layouts  1.93 us (5%)
  between operations  0.65 us (2%)
    pallas_call x1, Pallas kernels, body(): pl.pallas_call(functools.partial(kernel, count_x, count_y), out_shape=(ja...  31.8 us
    unnamed x4, local copies, waits for them, and re-layouts  1.93 us
    pallas_call x1, Pallas kernels, body(): pl.pallas_call(decode_kernel, out_shape=(jax.ShapeDtypeStruct((CHANNELS,...  1.09 us

profile of v2, /device:TPU:1, one launch (start us, length us, event | category | flops | bytes accessed | tf_op | source)
XLA Modules:
  0.0 35.5 jit_solution(229160193805724940)
XLA Ops:
  0.6 31.8 %shard_map.122 = (f32[7,32,128]{2,1,0:T(8,128)}, s32[128,8,128]{2,1,0:T(8,128)}) custom-call(bf16[26,32,512]{2,1,0:T(8,128)(2,1)} %volume.1, s32[1,32]{1,0:T(1,128)} %bitcast.8, s32[1,32]{1,0:T(1,128)} %bitcast.9, f32[8,208]{1,0:T(8,128)} %constant.16.clone.marks, bf16[288,832]{1,0:T(8,128)(2,1)} %constant.17.clone.pack_w, ...), custom_call_target="tpu_custom_call" | custom-call | tf_op jit(solution)/shard_map/pallas_call | solution.py:433
  32.5 0.0 copy-start
  32.5 1.0 %copy-done = s32[128,8,128]{2,1,0:T(8,128)S(1)} copy-done((s32[128,8,128]{2,1,0:T(8,128)S(1)}, s32[128,8,128]{2,1,0:T(8,128)}, u32[]{:S(2)}) %copy-start) | copy-done | bytes 524312
  33.5 0.0 copy-start.1
  33.5 0.9 %copy-done.1 = f32[7,32,128]{2,1,0:T(8,128)S(1)} copy-done((f32[7,32,128]{2,1,0:T(8,128)S(1)}, f32[7,32,128]{2,1,0:T(8,128)}, u32[]{:S(2)}) %copy-start.1) | copy-done | bytes 114712
  34.4 1.1 %shard_map.123 = (f32[7,256,128]{2,1,0:T(8,128)}, f32[7,32,128]{2,1,0:T(8,128)}) custom-call(s32[1024,128]{1,0:T(8,128)S(1)} %bitcast.7, f32[7,32,128]{2,1,0:T(8,128)S(1)} %copy-done.1), custom_call_target="tpu_custom_call" | custom-call | tf_op jit(solution)/shard_map/pallas_call | solution.py:462
Async XLA Ops:
  32.5 1.0 %copy-start = (s32[128,8,128]{2,1,0:T(8,128)S(1)}, s32[128,8,128]{2,1,0:T(8,128)}, u32[]{:S(2)}) copy-start(s32[128,8,128]{2,1,0:T(8,128)} %get-tuple-element.6) | copy-start | bytes 1572868
  33.5 0.9 %copy-start.1 = (f32[7,32,128]{2,1,0:T(8,128)S(1)}, f32[7,32,128]{2,1,0:T(8,128)}, u32[]{:S(2)}) copy-start(f32[7,32,128]{2,1,0:T(8,128)} %get-tuple-element.7.geometry_in) | copy-start | bytes 344068

commit v3 on v2

v3 whole, which is shorter than its diff:
```python
import functools
import math

import jax
import jax.numpy as jnp
import ml_dtypes
import numpy as np
from jax import lax
from jax.experimental import pallas as pl
from jax.experimental.pallas import tpu as pltpu
from jax.sharding import PartitionSpec as P

MESH = pl.DeviceIdType.MESH

raw_taps = [math.exp(-((offset - 4) ** 2) / 8.0) for offset in range(9)]
gauss_taps = np.array([value / sum(raw_taps) for value in raw_taps])
sharpness = 20.0
normal_floor = 0.01

PLANES_IN = 26
TILE_X = 32
TILE_Y = 512
OWN = PLANES_IN * TILE_X
REACH = 5
WIDE_X = TILE_X + 2
GROUPS = 3
GROUP_PLANES = 6
GROUP_IN = GROUP_PLANES + 8
INNER_X = 24
OUTER_X = 10
INNER = GROUP_PLANES * INNER_X
OUTER = 64
GROUP_ROWS = INNER + OUTER
SIDE_ROWS = 144
WINDOW = 96
WINDOW_AT = [(REACH * GROUP_PLANES * g) // 16 * 16 for g in range(GROUPS)]
WIDE_Y = TILE_Y + 128
ROWS = 32
CHANNELS = 7
LEVELS = 32766.0


def outer_place(x):
    if x < REACH:
        return x
    return x - INNER_X if x >= REACH + INNER_X else None


def row_of(plane, x):
    outer = outer_place(x)
    if outer is None:
        return plane * INNER_X + x - REACH
    return INNER + plane * OUTER_X + outer


def halves(matrix):
    high = matrix.astype(np.float32).astype(ml_dtypes.bfloat16)
    low = (matrix - high.astype(np.float64)).astype(np.float32).astype(ml_dtypes.bfloat16)
    return np.stack([high, low])


def pack_matrix():
    matrix = np.zeros((2 * SIDE_ROWS, OWN))
    for z in range(PLANES_IN):
        for i in range(REACH):
            matrix[z * REACH + i, z * TILE_X + i] = 1
            matrix[SIDE_ROWS + z * REACH + i, z * TILE_X + TILE_X - REACH + i] = 1
    return matrix.astype(ml_dtypes.bfloat16)


def column_matrices():
    take = np.zeros((32, 256))
    put = np.zeros((32, 128))
    for i in range(REACH):
        take[i, i] = 1
        take[16 + i, 256 - REACH + i] = 1
        put[i, 128 - REACH + i] = 1
        put[16 + i, i] = 1
    return take.astype(ml_dtypes.bfloat16), put.astype(ml_dtypes.bfloat16)


def tap(distance):
    return gauss_taps[distance + 4] if -4 <= distance <= 4 else 0.0


def own_matrix():
    matrix = np.zeros((GROUP_ROWS, GROUP_IN * TILE_X))
    for plane in range(GROUP_PLANES):
        for x in range(WIDE_X):
            for z in range(9):
                for source in range(TILE_X):
                    matrix[row_of(plane, x), (plane + z) * TILE_X + source] = (
                        gauss_taps[z] * tap(source - (x - 1))
                    )
    return halves(matrix)


def side_matrices():
    found = []
    for g in range(GROUPS):
        matrix = np.zeros((OUTER, 2 * WINDOW))
        for plane in range(GROUP_PLANES):
            for x in range(WIDE_X):
                outer = outer_place(x)
                if outer is None:
                    continue
                for z in range(9):
                    for i in range(REACH):
                        row = (g * GROUP_PLANES + plane + z) * REACH + i - WINDOW_AT[g]
                        out = plane * OUTER_X + outer
                        matrix[out, row] = gauss_taps[z] * tap(i - REACH - (x - 1))
                        matrix[out, WINDOW + row] = gauss_taps[z] * tap(TILE_X + i - (x - 1))
        found.append(halves(matrix))
    return np.stack(found)


def along_y_matrices():
    scale = -sharpness / math.log(2.0)
    main = np.zeros((512, 256))
    for out in range(256):
        for distance in range(-4, 5):
            main[128 + out + distance, out] = scale * tap(distance)
    edge = np.zeros((512, 128))
    for distance in range(-4, 5):
        edge[127 + distance, 0] = scale * tap(distance)
        edge[384 + distance, 1] = scale * tap(distance)
    return halves(main), halves(edge)


MEAN = np.array([0, 1, 1, 1, 1, 0]) / 4
FIRST = np.array([0, 1, 0, 0, 0, 0]) / 1
SOFT = np.array([1, 3, 4, 4, 3, 1]) / 16
SLOPE = np.array([-1, -1, 0, 0, 1, 1]) / 8


def cell_matrices():
    pairs = [(MEAN, MEAN), (FIRST, MEAN), (MEAN, FIRST), (SLOPE, SOFT), (SOFT, SLOPE), (SOFT, SOFT)]
    inner = np.zeros((len(pairs) * ROWS, GROUPS * INNER))
    outer = np.zeros((len(pairs) * ROWS, GROUPS * OUTER))
    for at, (along_z, along_x) in enumerate(pairs):
        for layer in range(4):
            for cell in range(8):
                for z in range(6):
                    for x in range(6):
                        group, plane = divmod(4 * layer + z, GROUP_PLANES)
                        row = row_of(plane, 4 * cell + x)
                        out = at * ROWS + layer * 8 + cell
                        weight = along_z[z] * along_x[x]
                        if row < INNER:
                            inner[out, group * INNER + row] += weight
                        else:
                            outer[out, group * OUTER + row - INNER] += weight
    return inner.astype(ml_dtypes.bfloat16), outer.astype(ml_dtypes.bfloat16)


def cell_y_matrix():
    matrix = np.zeros((2, TILE_Y + 128, 256))
    for at, weights in enumerate((MEAN, FIRST, SOFT, SLOPE)):
        for cell in range(128):
            for y in range(6):
                place = 4 * cell + y - 1
                row = TILE_Y if place < 0 else TILE_Y + 1 if place >= TILE_Y else place
                matrix[at // 2, row, at % 2 * 128 + cell] = weights[y]
    return matrix.astype(ml_dtypes.bfloat16)


def side_marks():
    marks = np.zeros((8, GROUPS * OUTER), np.float32)
    for group in range(GROUPS):
        for plane in range(GROUP_PLANES):
            marks[0, group * OUTER + plane * OUTER_X] = 1
            marks[1, group * OUTER + plane * OUTER_X + OUTER_X - 1] = 1
    return marks


def split(value):
    high = value.astype(jnp.bfloat16)
    return high, (value - high.astype(jnp.float32)).astype(jnp.bfloat16)


def dot(left, right):
    return jnp.dot(left, right, preferred_element_type=jnp.float32)


def routing(owner, flags):
    wide = (ROWS, ROWS)
    row = lax.broadcasted_iota(jnp.int32, wide, 0)
    column = lax.broadcasted_iota(jnp.int32, wide, 1)
    owner_across = jnp.broadcast_to(owner.astype(jnp.float32), wide)
    flag_across = jnp.broadcast_to(flags.astype(jnp.float32), wide)
    same = row == column
    owner_down = jnp.sum(jnp.where(same, owner_across, 0.0), axis=1, keepdims=True)
    flag_down = jnp.sum(jnp.where(same, flag_across, 0.0), axis=1, keepdims=True)
    earlier = (column < row) & (owner_down == owner_across)
    slot = jnp.sum(jnp.where(earlier, flag_across, 0.0), axis=1, keepdims=True)
    code = jnp.where(flag_down > 0.5, owner_down * 2.0 + slot, -8.0)
    place = lax.broadcasted_iota(jnp.int32, (ROWS, 256), 1)
    mine = (place & (ROWS - 1)) == lax.broadcasted_iota(jnp.int32, (ROWS, 256), 0)
    spread = jnp.sum(jnp.where(mine, code, 0.0), axis=0, keepdims=True)
    part = ((lax.broadcasted_iota(jnp.int32, (1, 256), 1) >> 5) & 3).astype(jnp.float32)
    return spread * 4.0 + part


def kernel(
    count_x, count_y,
    volume, owner, flags, marks, put_w,
    take_w, pack_w, own_w, main_w, edge_w, inner_w, side_w, outer_w, cell_y_w,
    geometry, arrived,
    tile, packed, columns, corners, sides, beside, corner_in, ends, side_ends,
    smooth, sharp, chosen, leaving,
    take_v, pack_v, own_v, main_v, edge_v, inner_v, side_v, outer_v, cell_y_v,
    load_sem, send_sem, recv_sem, far_sem, out_send, out_recv,
):
    p = lax.axis_index("gx")
    q = lax.axis_index("gy")
    count = count_x * count_y
    me = p * count_y + q

    def at(dx, dy):
        return (lax.rem(p + dx + count_x, count_x), lax.rem(q + dy + count_y, count_y))

    around = [(0, -1), (0, 1), (-1, 0), (1, 0), (-1, -1), (-1, 1), (1, -1), (1, 1)]
    barrier = pltpu.get_barrier_semaphore()
    pairs = [
        (volume, tile),
        (take_w, take_v),
        (pack_w, pack_v),
        (own_w, own_v),
        (main_w, main_v),
        (edge_w, edge_v),
        (inner_w, inner_v),
        (side_w, side_v),
        (outer_w, outer_v),
        (cell_y_w, cell_y_v),
    ]
    loads = [pltpu.make_async_copy(*pair, load_sem.at[i]) for i, pair in enumerate(pairs)]
    for load in loads:
        load.start()
    for dx, dy in around:
        pl.semaphore_signal(barrier, inc=1, device_id=at(dx, dy), device_id_type=MESH)

    def take_columns(rows):
        both = jnp.concatenate([rows[:, 0:128], rows[:, TILE_Y - 128 : TILE_Y]], axis=1)
        return lax.dot_general(
            take_v[...], both, (((1,), (1,)), ((), ())), preferred_element_type=jnp.float32
        ).astype(jnp.bfloat16)

    def put_columns(taken):
        return lax.dot_general(
            taken, put_w[...], (((0,), (0,)), ((), ())), preferred_element_type=jnp.float32
        ).astype(jnp.bfloat16)

    for load in loads[0:3]:
        load.wait()
    own = tile[...].reshape(OWN, TILE_Y)
    edge_rows = dot(pack_v[...], own).astype(jnp.bfloat16)
    packed[...] = edge_rows
    columns[:, 0:OWN] = take_columns(own)
    for side in range(2):
        corners[side, :, 0:SIDE_ROWS] = take_columns(
            edge_rows[side * SIDE_ROWS : (side + 1) * SIDE_ROWS]
        )

    pl.semaphore_wait(barrier, len(around))
    for dx, dy in around:
        pl.semaphore_signal(far_sem.at[0], inc=1, device_id=at(dx, dy), device_id_type=MESH)
    sends = []
    for i, (dx, dy) in enumerate(around):
        rows, rows_there = (0, SIDE_ROWS) if dx < 0 else (SIDE_ROWS, 0)
        lines, lines_there = (0, 16) if dy < 0 else (16, 0)
        if dx == 0:
            source = columns.at[pl.ds(lines, 16), :]
            target = beside.at[pl.ds(lines_there, 16), :]
        elif dy == 0:
            source = packed.at[pl.ds(rows, SIDE_ROWS), :]
            target = sides.at[pl.ds(rows_there, SIDE_ROWS), :]
        else:
            source = corners.at[rows // SIDE_ROWS, pl.ds(lines, 16), :]
            target = corner_in.at[rows_there // SIDE_ROWS, pl.ds(lines_there, 16), :]
        sends.append(
            pltpu.make_async_remote_copy(
                src_ref=source,
                dst_ref=target,
                send_sem=send_sem.at[i],
                recv_sem=recv_sem.at[i],
                device_id=at(dx, dy),
                device_id_type=MESH,
            )
        )
    for send in sends:
        send.start()

    loads[3].wait()
    for g in range(GROUPS):
        block = tile[g * GROUP_PLANES : g * GROUP_PLANES + GROUP_IN].reshape(
            GROUP_IN * TILE_X, TILE_Y
        )
        smooth[g, :, 128:WIDE_Y] = dot(own_v[0], block) + dot(own_v[1], block)

    codes = routing(owner[...], flags[...])
    number = lax.broadcasted_iota(jnp.int32, (count * 8, 256), 0).astype(jnp.float32)
    chosen[...] = jnp.where(number == codes, 1.0, 0.0).astype(jnp.bfloat16)

    pl.semaphore_wait(far_sem.at[0], len(around))
    for dx, dy in around:
        pl.semaphore_signal(
            far_sem.at[1], inc=1, device_id=at(2 * dx, 2 * dy), device_id_type=MESH
        )
    for load in loads[4:]:
        load.wait()
    for send in sends[0:2]:
        send.wait()

    @pl.when(q == 0)
    def _():
        beside[0:16, :] = jnp.zeros((16, beside.shape[1]), jnp.bfloat16)

    @pl.when(q == count_y - 1)
    def _():
        beside[16:32, :] = jnp.zeros((16, beside.shape[1]), jnp.bfloat16)

    lane = lax.broadcasted_iota(jnp.int32, (1, 128), 1)
    left_out = jnp.where(q == 0, 0, -1)
    right_out = jnp.where(q == count_y - 1, 1, -1)
    edge_keep = jnp.where((lane == left_out) | (lane == right_out), 0.0, 1.0)

    def sigmoid_of(power):
        below = 1.0 + jnp.exp2(jnp.minimum(power, 126.0))
        guess = pl.reciprocal(below, approx=True)
        return guess * (2.0 - below * guess)

    def indicator(blurred):
        high, low = split(blurred)

        def along_y(choose, weights):
            high_part = choose(high)
            return sigmoid_of(
                dot(high_part, weights[0])
                + dot(choose(low), weights[0])
                + dot(high_part, weights[1])
            )

        def last(part):
            return jnp.concatenate([part[:, 256:WIDE_Y], part[:, 0:128]], axis=1)

        def ends_of(part):
            return jnp.concatenate([part[:, 0:256], part[:, 512:WIDE_Y], part[:, 0:128]], axis=1)

        return split(
            jnp.concatenate(
                [
                    along_y(lambda part: part[:, 0:512], main_v),
                    along_y(last, main_v),
                    edge_keep * along_y(ends_of, edge_v),
                ],
                axis=1,
            )
        )

    ends[...] = put_columns(beside[:, 0:OWN])
    for g in range(GROUPS):
        first = g * GROUP_PLANES * TILE_X
        block = ends[first : first + GROUP_IN * TILE_X, :]
        smooth[g, :, 0:128] = dot(own_v[0], block) + dot(own_v[1], block)
        high, low = indicator(smooth[g, 0:INNER, :])
        sharp[0, g * INNER : (g + 1) * INNER, :] = high
        sharp[1, g * INNER : (g + 1) * INNER, :] = low
    cells = dot(inner_v[...], sharp[0]) + dot(inner_v[...], sharp[1])

    pl.semaphore_wait(far_sem.at[1], len(around))
    for dx in (-4, 4):
        pl.semaphore_signal(far_sem.at[2], inc=1, device_id=at(dx, 0), device_id_type=MESH)
    for send in sends[2:]:
        send.wait()

    @pl.when(p == 0)
    def _():
        sides[0:SIDE_ROWS, :] = jnp.zeros((SIDE_ROWS, TILE_Y), jnp.bfloat16)
        corner_in[0] = jnp.zeros(corner_in.shape[1:], jnp.bfloat16)

    @pl.when(p == count_x - 1)
    def _():
        sides[SIDE_ROWS : 2 * SIDE_ROWS, :] = jnp.zeros((SIDE_ROWS, TILE_Y), jnp.bfloat16)
        corner_in[1] = jnp.zeros(corner_in.shape[1:], jnp.bfloat16)

    @pl.when(q == 0)
    def _():
        corner_in[:, 0:16, :] = jnp.zeros((2, 16, corner_in.shape[2]), jnp.bfloat16)

    @pl.when(q == count_y - 1)
    def _():
        corner_in[:, 16:32, :] = jnp.zeros((2, 16, corner_in.shape[2]), jnp.bfloat16)

    for side in range(2):
        side_ends[side * SIDE_ROWS : (side + 1) * SIDE_ROWS, :] = put_columns(
            corner_in[side, :, 0:SIDE_ROWS]
        )
    blurred = []
    for g in range(GROUPS):
        low_rows = slice(WINDOW_AT[g], WINDOW_AT[g] + WINDOW)
        high_rows = slice(SIDE_ROWS + WINDOW_AT[g], SIDE_ROWS + WINDOW_AT[g] + WINDOW)
        window = jnp.concatenate(
            [
                jnp.concatenate([side_ends[low_rows, :], sides[low_rows, :]], axis=1),
                jnp.concatenate([side_ends[high_rows, :], sides[high_rows, :]], axis=1),
            ],
            axis=0,
        )
        blurred.append(
            dot(side_v[g, 0], window) + dot(side_v[g, 1], window) + smooth[g, INNER:GROUP_ROWS, :]
        )
    high, low = indicator(jnp.concatenate(blurred, axis=0))
    low_out = jnp.where(p == 0, 1.0, 0.0)
    high_out = jnp.where(p == count_x - 1, 1.0, 0.0)
    keep = (1.0 - low_out * marks[0:1, :] - high_out * marks[1:2, :]).astype(jnp.bfloat16)
    weights = outer_v[...] * keep
    cells = cells + dot(weights, high) + dot(weights, low)

    high, low = split(cells)
    plain = dot(high[0:96], cell_y_v[0]) + dot(low[0:96], cell_y_v[0])
    slopes = dot(high[96:192], cell_y_v[1]) + dot(low[96:192], cell_y_v[1])
    mean_z, mean_x, mean_y = slopes[0:32, 0:128], slopes[32:64, 0:128], slopes[64:96, 128:256]
    shrink = -lax.rsqrt(mean_z * mean_z + mean_x * mean_x + mean_y * mean_y + normal_floor)
    found = [
        plain[0:32, 0:128],
        plain[32:64, 0:128],
        plain[64:96, 0:128],
        plain[0:32, 128:256],
        mean_z * shrink,
        mean_x * shrink,
        mean_y * shrink,
    ]
    for channel in range(CHANNELS):
        geometry[channel] = found[channel]

    most = functools.reduce(jnp.maximum, [jnp.abs(value) for value in found])
    most = jnp.maximum(jnp.max(most, axis=1, keepdims=True), 1e-37)
    grade = jnp.ceil(8.0 * jnp.log2(most) + 0.02)
    stretch = jnp.exp2(grade * -0.125)
    whole = [jnp.floor(value * stretch * LEVELS + 0.5) for value in found]
    whole.append(jnp.broadcast_to(grade, (ROWS, 128)))
    coded = jnp.concatenate(
        [jnp.concatenate(whole[0:4], axis=0), jnp.concatenate(whole[4:8], axis=0)], axis=1
    )
    upper = jnp.floor(coded * (1.0 / 256.0) + 0.5) * 256.0
    stacked = jnp.concatenate([upper, coded - upper], axis=0).astype(jnp.bfloat16)
    placed = dot(chosen[...], stacked).astype(jnp.int32)
    joined = (placed[:, 128:256] << 16) | (placed[:, 0:128] & 0xFFFF)
    leaving[...] = joined.reshape(count, 8, 128)

    pl.semaphore_wait(far_sem.at[2], 2)

    def send_out(step, carry):
        other = lax.rem(me + step, count)
        pltpu.make_async_remote_copy(
            src_ref=leaving.at[other],
            dst_ref=arrived.at[me],
            send_sem=out_send,
            recv_sem=out_recv,
            device_id=(other // count_y, lax.rem(other, count_y)),
            device_id_type=MESH,
        ).start()
        return carry

    lax.fori_loop(1, count, send_out, 0)
    arrived[me] = leaving[me]
    others = pl.ds(0, count - 1)
    every = pltpu.make_async_remote_copy(
        src_ref=leaving.at[others],
        dst_ref=arrived.at[others],
        send_sem=out_send,
        recv_sem=out_recv,
        device_id=at(1, 0),
        device_id_type=MESH,
    )
    every.wait_send()
    every.wait_recv()


def decode_kernel(
    coded, geometry_in, received, geometry, coded_v, geometry_v, received_v,
    copy_sem, load_sem, store_sem,
):
    pieces = load_sem.shape[0]
    rows = received_v.shape[1] // pieces
    whole_in = pltpu.make_async_copy(geometry_in, geometry_v, copy_sem.at[0])
    whole_out = pltpu.make_async_copy(geometry_v, geometry, copy_sem.at[1])
    loads, stores = [], []
    for i in range(pieces):
        source = pl.ds(i * rows * 4, rows * 4)
        target = pl.ds(i * rows, rows)
        loads.append(
            pltpu.make_async_copy(coded.at[source, :], coded_v.at[source, :], load_sem.at[i])
        )
        stores.append(
            pltpu.make_async_copy(
                received_v.at[:, target, :], received.at[:, target, :], store_sem.at[i]
            )
        )
    for load in loads:
        load.start()
    whole_in.start()
    for i in range(pieces):
        loads[i].wait()
        target = slice(i * rows, (i + 1) * rows)

        def pair(part):
            both = coded_v[pl.ds(i * rows * 4 + part, rows, stride=4), :]
            return (both << 16) >> 16, both >> 16

        fourth, grade = pair(3)
        scale = jnp.exp2(grade.astype(jnp.float32) * 0.125) * (1.0 / LEVELS)
        received_v[3, target] = fourth.astype(jnp.float32) * scale
        for part in range(3):
            low, high = pair(part)
            received_v[part, target] = low.astype(jnp.float32) * scale
            received_v[part + 4, target] = high.astype(jnp.float32) * scale
        stores[i].start()
    whole_in.wait()
    whole_out.start()
    for store in stores:
        store.wait()
    whole_out.wait()


def body(count_x, count_y, volume, owner, flags):
    count = count_x * count_y
    main_w, edge_w = along_y_matrices()
    inner_w, outer_w = cell_matrices()
    take_w, put_w = column_matrices()
    weights = [
        take_w, pack_matrix(), own_matrix(), main_w, edge_w, inner_w, side_matrices(), outer_w, cell_y_matrix(),
    ]
    in_vmem = pl.BlockSpec(memory_space=pltpu.VMEM)
    anywhere = pl.BlockSpec(memory_space=pl.ANY)
    bf16 = jnp.bfloat16
    geometry, arrived = pl.pallas_call(
        functools.partial(kernel, count_x, count_y),
        out_shape=(
            jax.ShapeDtypeStruct((CHANNELS, ROWS, 128), jnp.float32),
            jax.ShapeDtypeStruct((count, 8, 128), jnp.int32),
        ),
        in_specs=[anywhere] + [in_vmem] * 4 + [anywhere] * len(weights),
        out_specs=(in_vmem, in_vmem),
        scratch_shapes=[
            pltpu.VMEM((PLANES_IN, TILE_X, TILE_Y), bf16),
            pltpu.VMEM((2 * SIDE_ROWS, TILE_Y), bf16),
            pltpu.VMEM((32, 896), bf16),
            pltpu.VMEM((2, 32, 256), bf16),
            pltpu.VMEM((2 * SIDE_ROWS, TILE_Y), bf16),
            pltpu.VMEM((32, 896), bf16),
            pltpu.VMEM((2, 32, 256), bf16),
            pltpu.VMEM((OWN, 128), bf16),
            pltpu.VMEM((2 * SIDE_ROWS, 128), bf16),
            pltpu.VMEM((GROUPS, GROUP_ROWS, WIDE_Y), jnp.float32),
            pltpu.VMEM((2, GROUPS * INNER, WIDE_Y), bf16),
            pltpu.VMEM((count * 8, 256), bf16),
            pltpu.VMEM((count, 8, 128), jnp.int32),
        ]
        + [pltpu.VMEM(weight.shape, bf16) for weight in weights]
        + [
            pltpu.SemaphoreType.DMA((1 + len(weights),)),
            pltpu.SemaphoreType.DMA((8,)),
            pltpu.SemaphoreType.DMA((8,)),
            pltpu.SemaphoreType.REGULAR((3,)),
            pltpu.SemaphoreType.DMA,
            pltpu.SemaphoreType.DMA,
        ],
        compiler_params=pltpu.CompilerParams(
            collective_id=0, has_side_effects=True, vmem_limit_bytes=62 * 2**20
        ),
    )(volume, owner.reshape(1, ROWS), flags.reshape(1, ROWS), side_marks(), put_w, *weights)
    pieces = 4
    received, geometry = pl.pallas_call(
        decode_kernel,
        out_shape=(
            jax.ShapeDtypeStruct((CHANNELS, count * 2, 128), jnp.float32),
            jax.ShapeDtypeStruct(geometry.shape, jnp.float32),
        ),
        in_specs=[anywhere, anywhere],
        out_specs=(anywhere, anywhere),
        scratch_shapes=[
            pltpu.VMEM((count * 8, 128), jnp.int32),
            pltpu.VMEM(geometry.shape, jnp.float32),
            pltpu.VMEM((CHANNELS, count * 2, 128), jnp.float32),
            pltpu.SemaphoreType.DMA((2,)),
            pltpu.SemaphoreType.DMA((pieces,)),
            pltpu.SemaphoreType.DMA((pieces,)),
        ],
        compiler_params=pltpu.CompilerParams(vmem_limit_bytes=62 * 2**20),
    )(arrived.reshape(count * 8, 128), geometry)
    received = jnp.transpose(received, (1, 0, 2))[None]
    return (geometry.reshape(CHANNELS, 4, 8, 128), received)


def solution(mesh):
    in_specs = (P(None, "gx", "gy"), P("gx", "gy", None, None), P("gx", "gy", None))
    out_specs = (P(None, None, "gx", "gy"), P(("gx", "gy"), None, None, None))
    return jax.shard_map(
        functools.partial(body, mesh.shape["gx"], mesh.shape["gy"]),
        mesh=mesh,
        in_specs=in_specs,
        out_specs=out_specs,
        check_vma=False,
    )
```

time: 35.7 us -> 31.4 us (0.88)
  Pallas kernels: 32.9 us -> 30.5 us
  local copies, waits for them, and re-layouts: 1.93 us -> 0 us
    pallas_call x1, Pallas kernels: 31.8 us -> 28.5 us  [body(): pl.pallas_call(functools.partial(kernel, count_x, count_y), out_shape=(ja...]
    unnamed x4 -> x0, local copies, waits for them, and re-layouts: 1.93 us -> none
    pallas_call x1, Pallas kernels: 1.09 us -> 1.97 us  [body(): pl.pallas_call(decode_kernel, out_shape=(jax.ShapeDtypeStruct((CHANNELS,...]
where the time goes in v3:
time: 31.4 us; the launch traced here: 31.1 us
  Pallas kernels  30.5 us (97%)
  between operations  0.64 us (2%)
    pallas_call x1, Pallas kernels, body(): pl.pallas_call(functools.partial(kernel, count_x, count_y), out_shape=(ja...  28.5 us
    pallas_call x1, Pallas kernels, body(): pl.pallas_call(decode_kernel, out_shape=(jax.ShapeDtypeStruct((CHANNELS,...  1.97 us

profile of v3, /device:TPU:1, one launch (start us, length us, event | category | flops | bytes accessed | tf_op | source)
XLA Modules:
  0.0 31.1 jit_solution(3349148142180415419)
XLA Ops:
  0.6 28.5 %shard_map.149 = (f32[7,32,128]{2,1,0:T(8,128)}, s32[128,8,128]{2,1,0:T(8,128)}) custom-call(bf16[26,32,512]{2,1,0:T(8,128)(2,1)} %volume.1, s32[1,32]{1,0:T(1,128)} %bitcast.8, s32[1,32]{1,0:T(1,128)} %bitcast.9, f32[8,192]{1,0:T(8,128)} %constant.22.clone.marks, bf16[32,128]{1,0:T(8,128)(2,1)} %constant.23.clone.put_w, ...), custom_call_target="tpu_custom_call" | custom-call | tf_op jit(solution)/shard_map/pallas_call | solution.py:537
  29.1 2.0 %shard_map.150 = (f32[7,256,128]{2,1,0:T(8,128)}, f32[7,32,128]{2,1,0:T(8,128)}) custom-call(s32[1024,128]{1,0:T(8,128)} %bitcast.7, f32[7,32,128]{2,1,0:T(8,128)} %get-tuple-element.7.geometry_in), custom_call_target="tpu_custom_call" | custom-call | tf_op jit(solution)/shard_map/pallas_call | solution.py:574

commit v4 on v3

--- a/solution.py
+++ b/solution.py
@@ -34,7 +34,10 @@
 SIDE_ROWS = 144
 WINDOW = 96
 WINDOW_AT = [(REACH * GROUP_PLANES * g) // 16 * 16 for g in range(GROUPS)]
+PACK_PLANES = 8
+PACK_ROWS = PACK_PLANES * REACH
 WIDE_Y = TILE_Y + 128
+BAND = (112, 400)
 ROWS = 32
 CHANNELS = 7
 LEVELS = 32766.0
@@ -60,11 +63,11 @@
 
 
 def pack_matrix():
-    matrix = np.zeros((2 * SIDE_ROWS, OWN))
-    for z in range(PLANES_IN):
+    matrix = np.zeros((2 * PACK_ROWS, PACK_PLANES * TILE_X))
+    for z in range(PACK_PLANES):
         for i in range(REACH):
             matrix[z * REACH + i, z * TILE_X + i] = 1
-            matrix[SIDE_ROWS + z * REACH + i, z * TILE_X + TILE_X - REACH + i] = 1
+            matrix[PACK_ROWS + z * REACH + i, z * TILE_X + TILE_X - REACH + i] = 1
     return matrix.astype(ml_dtypes.bfloat16)
 
 
@@ -114,17 +117,13 @@
     return np.stack(found)
 
 
-def along_y_matrices():
+def along_y_matrix():
     scale = -sharpness / math.log(2.0)
     main = np.zeros((512, 256))
     for out in range(256):
         for distance in range(-4, 5):
             main[128 + out + distance, out] = scale * tap(distance)
-    edge = np.zeros((512, 128))
-    for distance in range(-4, 5):
-        edge[127 + distance, 0] = scale * tap(distance)
-        edge[384 + distance, 1] = scale * tap(distance)
-    return halves(main), halves(edge)
+    return halves(main)[:, BAND[0] : BAND[1]]
 
 
 MEAN = np.array([0, 1, 1, 1, 1, 0]) / 4
@@ -159,7 +158,7 @@
         for cell in range(128):
             for y in range(6):
                 place = 4 * cell + y - 1
-                row = TILE_Y if place < 0 else TILE_Y + 1 if place >= TILE_Y else place
+                row = TILE_Y + 127 if place < 0 else place
                 matrix[at // 2, row, at % 2 * 128 + cell] = weights[y]
     return matrix.astype(ml_dtypes.bfloat16)
 
@@ -203,13 +202,13 @@
 
 def kernel(
     count_x, count_y,
-    volume, owner, flags, marks, put_w,
-    take_w, pack_w, own_w, main_w, edge_w, inner_w, side_w, outer_w, cell_y_w,
-    geometry, arrived,
+    volume, owner_h, flags_h, marks_h,
+    take_w, pack_w, own_w, main_w, put_w, inner_w, side_w, outer_w, cell_y_w,
+    geometry_h, arrived,
     tile, packed, columns, corners, sides, beside, corner_in, ends, side_ends,
-    smooth, sharp, chosen, leaving,
-    take_v, pack_v, own_v, main_v, edge_v, inner_v, side_v, outer_v, cell_y_v,
-    load_sem, send_sem, recv_sem, far_sem, out_send, out_recv,
+    smooth, sharp, chosen, leaving, geometry, owner, flags, marks, main_v,
+    take_v, pack_v, own_v, put_v, inner_v, side_v, outer_v, cell_y_v,
+    load_sem, send_sem, recv_sem, far_sem, out_send, out_recv, own_sem, geometry_sem,
 ):
     p = lax.axis_index("gx")
     q = lax.axis_index("gy")
@@ -221,23 +220,28 @@
 
     around = [(0, -1), (0, 1), (-1, 0), (1, 0), (-1, -1), (-1, 1), (1, -1), (1, 1)]
     barrier = pltpu.get_barrier_semaphore()
+    for dx, dy in around:
+        pl.semaphore_signal(barrier, inc=1, device_id=at(dx, dy), device_id_type=MESH)
     pairs = [
         (volume, tile),
+        (pack_w, pack_v),
         (take_w, take_v),
-        (pack_w, pack_v),
         (own_w, own_v),
-        (main_w, main_v),
-        (edge_w, edge_v),
+        (owner_h, owner),
+        (flags_h, flags),
+        (put_w, put_v),
+        (main_w, main_v.at[:, pl.ds(BAND[0], BAND[1] - BAND[0]), :]),
         (inner_w, inner_v),
         (side_w, side_v),
+        (marks_h, marks),
         (outer_w, outer_v),
         (cell_y_w, cell_y_v),
     ]
     loads = [pltpu.make_async_copy(*pair, load_sem.at[i]) for i, pair in enumerate(pairs)]
-    for load in loads:
+    for load in loads[0:4]:
         load.start()
-    for dx, dy in around:
-        pl.semaphore_signal(barrier, inc=1, device_id=at(dx, dy), device_id_type=MESH)
+    main_v[:, 0 : BAND[0], :] = jnp.zeros((2, BAND[0], 256), jnp.bfloat16)
+    main_v[:, BAND[1] : 512, :] = jnp.zeros((2, 512 - BAND[1], 256), jnp.bfloat16)
 
     def take_columns(rows):
         both = jnp.concatenate([rows[:, 0:128], rows[:, TILE_Y - 128 : TILE_Y]], axis=1)
@@ -247,13 +251,22 @@
 
     def put_columns(taken):
         return lax.dot_general(
-            taken, put_w[...], (((0,), (0,)), ((), ())), preferred_element_type=jnp.float32
+            taken, put_v[...], (((0,), (0,)), ((), ())), preferred_element_type=jnp.float32
         ).astype(jnp.bfloat16)
 
     for load in loads[0:3]:
         load.wait()
+    for load in loads[4:]:
+        load.start()
     own = tile[...].reshape(OWN, TILE_Y)
-    edge_rows = dot(pack_v[...], own).astype(jnp.bfloat16)
+    low_rows, high_rows = [], []
+    for first in range(0, PLANES_IN, PACK_PLANES):
+        block = own[first * TILE_X : min(first + PACK_PLANES, PLANES_IN) * TILE_X]
+        taken = dot(pack_v[:, 0 : block.shape[0]], block)
+        rows = min(PACK_ROWS, SIDE_ROWS - first * REACH)
+        low_rows.append(taken[0:rows])
+        high_rows.append(taken[PACK_ROWS : PACK_ROWS + rows])
+    edge_rows = jnp.concatenate(low_rows + high_rows, axis=0).astype(jnp.bfloat16)
     packed[...] = edge_rows
     columns[:, 0:OWN] = take_columns(own)
     for side in range(2):
@@ -262,7 +275,8 @@
         )
 
     pl.semaphore_wait(barrier, len(around))
-    for dx, dy in around:
+    diagonals = around[4:]
+    for dx, dy in diagonals:
         pl.semaphore_signal(far_sem.at[0], inc=1, device_id=at(dx, dy), device_id_type=MESH)
     sends = []
     for i, (dx, dy) in enumerate(around):
@@ -297,16 +311,18 @@
         )
         smooth[g, :, 128:WIDE_Y] = dot(own_v[0], block) + dot(own_v[1], block)
 
+    for load in loads[4:6]:
+        load.wait()
     codes = routing(owner[...], flags[...])
     number = lax.broadcasted_iota(jnp.int32, (count * 8, 256), 0).astype(jnp.float32)
     chosen[...] = jnp.where(number == codes, 1.0, 0.0).astype(jnp.bfloat16)
 
-    pl.semaphore_wait(far_sem.at[0], len(around))
-    for dx, dy in around:
+    pl.semaphore_wait(far_sem.at[0], len(diagonals))
+    for dx, dy in diagonals:
         pl.semaphore_signal(
             far_sem.at[1], inc=1, device_id=at(2 * dx, 2 * dy), device_id_type=MESH
         )
-    for load in loads[4:]:
+    for load in loads[6:]:
         load.wait()
     for send in sends[0:2]:
         send.wait()
@@ -320,8 +336,8 @@
         beside[16:32, :] = jnp.zeros((16, beside.shape[1]), jnp.bfloat16)
 
     lane = lax.broadcasted_iota(jnp.int32, (1, 128), 1)
-    left_out = jnp.where(q == 0, 0, -1)
-    right_out = jnp.where(q == count_y - 1, 1, -1)
+    left_out = jnp.where(q == 0, 127, -1)
+    right_out = jnp.where(q == count_y - 1, 0, -1)
     edge_keep = jnp.where((lane == left_out) | (lane == right_out), 0.0, 1.0)
 
     def sigmoid_of(power):
@@ -334,7 +350,7 @@
 
         def along_y(choose, weights):
             high_part = choose(high)
-            return sigmoid_of(
+            return (
                 dot(high_part, weights[0])
                 + dot(choose(low), weights[0])
                 + dot(high_part, weights[1])
@@ -343,15 +359,18 @@
         def last(part):
             return jnp.concatenate([part[:, 256:WIDE_Y], part[:, 0:128]], axis=1)
 
-        def ends_of(part):
-            return jnp.concatenate([part[:, 0:256], part[:, 512:WIDE_Y], part[:, 0:128]], axis=1)
-
+        def right_end(part):
+            return jnp.concatenate([part[:, 512:WIDE_Y], part[:, 0:128]], axis=1)
+
+        left = along_y(lambda part: part[:, 0:256], main_v[:, 128:384, 0:128])
+        right = along_y(right_end, main_v[:, 128:384, 128:256])
+        edge = jnp.where(lane == 127, left, right)
         return split(
             jnp.concatenate(
                 [
-                    along_y(lambda part: part[:, 0:512], main_v),
-                    along_y(last, main_v),
-                    edge_keep * along_y(ends_of, edge_v),
+                    sigmoid_of(along_y(lambda part: part[:, 0:512], main_v[...])),
+                    sigmoid_of(along_y(last, main_v[...])),
+                    edge_keep * sigmoid_of(edge),
                 ],
                 axis=1,
             )
@@ -367,7 +386,7 @@
         sharp[1, g * INNER : (g + 1) * INNER, :] = low
     cells = dot(inner_v[...], sharp[0]) + dot(inner_v[...], sharp[1])
 
-    pl.semaphore_wait(far_sem.at[1], len(around))
+    pl.semaphore_wait(far_sem.at[1], len(diagonals))
     for dx in (-4, 4):
         pl.semaphore_signal(far_sem.at[2], inc=1, device_id=at(dx, 0), device_id_type=MESH)
     for send in sends[2:]:
@@ -432,6 +451,8 @@
     ]
     for channel in range(CHANNELS):
         geometry[channel] = found[channel]
+    write = pltpu.make_async_copy(geometry, geometry_h, geometry_sem)
+    write.start()
 
     most = functools.reduce(jnp.maximum, [jnp.abs(value) for value in found])
     most = jnp.maximum(jnp.max(most, axis=1, keepdims=True), 1e-37)
@@ -463,7 +484,8 @@
         return carry
 
     lax.fori_loop(1, count, send_out, 0)
-    arrived[me] = leaving[me]
+    stay = pltpu.make_async_copy(leaving.at[me], arrived.at[me], own_sem)
+    stay.start()
     others = pl.ds(0, count - 1)
     every = pltpu.make_async_remote_copy(
         src_ref=leaving.at[others],
@@ -475,6 +497,8 @@
     )
     every.wait_send()
     every.wait_recv()
+    stay.wait()
+    write.wait()
 
 
 def decode_kernel(
@@ -525,23 +549,22 @@
 
 def body(count_x, count_y, volume, owner, flags):
     count = count_x * count_y
-    main_w, edge_w = along_y_matrices()
     inner_w, outer_w = cell_matrices()
     take_w, put_w = column_matrices()
     weights = [
-        take_w, pack_matrix(), own_matrix(), main_w, edge_w, inner_w, side_matrices(), outer_w, cell_y_matrix(),
+        take_w, pack_matrix(), own_matrix(), along_y_matrix(), put_w, inner_w, side_matrices(), outer_w, cell_y_matrix(),
     ]
-    in_vmem = pl.BlockSpec(memory_space=pltpu.VMEM)
     anywhere = pl.BlockSpec(memory_space=pl.ANY)
     bf16 = jnp.bfloat16
+    marks = side_marks()
     geometry, arrived = pl.pallas_call(
         functools.partial(kernel, count_x, count_y),
         out_shape=(
             jax.ShapeDtypeStruct((CHANNELS, ROWS, 128), jnp.float32),
             jax.ShapeDtypeStruct((count, 8, 128), jnp.int32),
         ),
-        in_specs=[anywhere] + [in_vmem] * 4 + [anywhere] * len(weights),
-        out_specs=(in_vmem, in_vmem),
+        in_specs=[anywhere] * (4 + len(weights)),
+        out_specs=(anywhere, anywhere),
         scratch_shapes=[
             pltpu.VMEM((PLANES_IN, TILE_X, TILE_Y), bf16),
             pltpu.VMEM((2 * SIDE_ROWS, TILE_Y), bf16),
@@ -556,20 +579,27 @@
             pltpu.VMEM((2, GROUPS * INNER, WIDE_Y), bf16),
             pltpu.VMEM((count * 8, 256), bf16),
             pltpu.VMEM((count, 8, 128), jnp.int32),
+            pltpu.VMEM((CHANNELS, ROWS, 128), jnp.float32),
+            pltpu.VMEM((1, ROWS), jnp.int32),
+            pltpu.VMEM((1, ROWS), jnp.int32),
+            pltpu.VMEM(marks.shape, jnp.float32),
+            pltpu.VMEM((2, 512, 256), bf16),
         ]
-        + [pltpu.VMEM(weight.shape, bf16) for weight in weights]
+        + [pltpu.VMEM(weight.shape, bf16) for weight in weights if weight is not weights[3]]
         + [
-            pltpu.SemaphoreType.DMA((1 + len(weights),)),
+            pltpu.SemaphoreType.DMA((4 + len(weights),)),
             pltpu.SemaphoreType.DMA((8,)),
             pltpu.SemaphoreType.DMA((8,)),
             pltpu.SemaphoreType.REGULAR((3,)),
+            pltpu.SemaphoreType.DMA,
+            pltpu.SemaphoreType.DMA,
             pltpu.SemaphoreType.DMA,
             pltpu.SemaphoreType.DMA,
         ],
         compiler_params=pltpu.CompilerParams(
             collective_id=0, has_side_effects=True, vmem_limit_bytes=62 * 2**20
         ),
-    )(volume, owner.reshape(1, ROWS), flags.reshape(1, ROWS), side_marks(), put_w, *weights)
+    )(volume, owner.reshape(1, ROWS), flags.reshape(1, ROWS), marks, *weights)
     pieces = 4
     received, geometry = pl.pallas_call(
         decode_kernel,

time: 31.4 us -> 30.2 us (0.962)
  Pallas kernels: 30.5 us -> 29.4 us
    pallas_call x1, Pallas kernels: 28.5 us -> 27.5 us  [body(): pl.pallas_call(functools.partial(kernel, count_x, count_y), out_shape=(ja...]
where the time goes in v4:
time: 30.2 us; the launch traced here: 30.1 us
  Pallas kernels  29.4 us (97%)
  between operations  0.64 us (2%)
    pallas_call x1, Pallas kernels, body(): pl.pallas_call(functools.partial(kernel, count_x, count_y), out_shape=(ja...  27.5 us
    pallas_call x1, Pallas kernels, body(): pl.pallas_call(decode_kernel, out_shape=(jax.ShapeDtypeStruct((CHANNELS,...  1.97 us

profile of v4, /device:TPU:1, one launch (start us, length us, event | category | flops | bytes accessed | tf_op | source)
XLA Modules:
  0.0 30.1 jit_solution(105158554932064336)
XLA Ops:
  0.6 27.5 %shard_map.140 = (f32[7,32,128]{2,1,0:T(8,128)}, s32[128,8,128]{2,1,0:T(8,128)}) custom-call(bf16[26,32,512]{2,1,0:T(8,128)(2,1)} %volume.1, s32[1,32]{1,0:T(1,128)} %bitcast.8, s32[1,32]{1,0:T(1,128)} %bitcast.9, f32[8,192]{1,0:T(8,128)} %constant.20.clone.marks_h, bf16[32,256]{1,0:T(8,128)(2,1)} %constant.21.clone.take_w, ...), custom_call_target="tpu_custom_call" | custom-call | tf_op jit(solution)/shard_map/pallas_call | solution.py:560
  28.1 2.0 %shard_map.141 = (f32[7,256,128]{2,1,0:T(8,128)}, f32[7,32,128]{2,1,0:T(8,128)}) custom-call(s32[1024,128]{1,0:T(8,128)} %bitcast.7, f32[7,32,128]{2,1,0:T(8,128)} %get-tuple-element.7.geometry_in), custom_call_target="tpu_custom_call" | custom-call | tf_op jit(solution)/shard_map/pallas_call | solution.py:604

commit v5 on v4

--- a/solution.py
+++ b/solution.py
@@ -502,34 +502,25 @@
 
 
 def decode_kernel(
-    coded, geometry_in, received, geometry, coded_v, geometry_v, received_v,
-    copy_sem, load_sem, store_sem,
+    coded, geometry_in, received, geometry, received_v, copy_sem, store_sem
 ):
-    pieces = load_sem.shape[0]
+    pieces = store_sem.shape[0]
     rows = received_v.shape[1] // pieces
-    whole_in = pltpu.make_async_copy(geometry_in, geometry_v, copy_sem.at[0])
-    whole_out = pltpu.make_async_copy(geometry_v, geometry, copy_sem.at[1])
-    loads, stores = [], []
+    whole = pltpu.make_async_copy(geometry_in, geometry, copy_sem)
+    whole.start()
+    stores = []
     for i in range(pieces):
-        source = pl.ds(i * rows * 4, rows * 4)
         target = pl.ds(i * rows, rows)
-        loads.append(
-            pltpu.make_async_copy(coded.at[source, :], coded_v.at[source, :], load_sem.at[i])
-        )
         stores.append(
             pltpu.make_async_copy(
                 received_v.at[:, target, :], received.at[:, target, :], store_sem.at[i]
             )
         )
-    for load in loads:
-        load.start()
-    whole_in.start()
     for i in range(pieces):
-        loads[i].wait()
         target = slice(i * rows, (i + 1) * rows)
 
         def pair(part):
-            both = coded_v[pl.ds(i * rows * 4 + part, rows, stride=4), :]
+            both = coded[pl.ds(i * rows * 4 + part, rows, stride=4), :]
             return (both << 16) >> 16, both >> 16
 
         fourth, grade = pair(3)
@@ -540,11 +531,9 @@
             received_v[part, target] = low.astype(jnp.float32) * scale
             received_v[part + 4, target] = high.astype(jnp.float32) * scale
         stores[i].start()
-    whole_in.wait()
-    whole_out.start()
     for store in stores:
         store.wait()
-    whole_out.wait()
+    whole.wait()
 
 
 def body(count_x, count_y, volume, owner, flags):
@@ -557,11 +546,14 @@
     anywhere = pl.BlockSpec(memory_space=pl.ANY)
     bf16 = jnp.bfloat16
     marks = side_marks()
+    operands = [volume, owner.reshape(1, ROWS), flags.reshape(1, ROWS), marks, *weights]
+    operands = [jnp.asarray(value) for value in operands]
+    in_vmem = pl.BlockSpec(memory_space=pltpu.VMEM)
     geometry, arrived = pl.pallas_call(
         functools.partial(kernel, count_x, count_y),
         out_shape=(
-            jax.ShapeDtypeStruct((CHANNELS, ROWS, 128), jnp.float32),
-            jax.ShapeDtypeStruct((count, 8, 128), jnp.int32),
+            pltpu.VMEM((CHANNELS, ROWS, 128), jnp.float32),
+            pltpu.VMEM((count, 8, 128), jnp.int32),
         ),
         in_specs=[anywhere] * (4 + len(weights)),
         out_specs=(anywhere, anywhere),
@@ -597,9 +589,9 @@
             pltpu.SemaphoreType.DMA,
         ],
         compiler_params=pltpu.CompilerParams(
-            collective_id=0, has_side_effects=True, vmem_limit_bytes=62 * 2**20
+            collective_id=0, has_side_effects=True, vmem_limit_bytes=40 * 2**20
         ),
-    )(volume, owner.reshape(1, ROWS), flags.reshape(1, ROWS), marks, *weights)
+    )(*[pltpu.with_memory_space_constraint(value, pltpu.HBM) for value in operands])
     pieces = 4
     received, geometry = pl.pallas_call(
         decode_kernel,
@@ -607,17 +599,14 @@
             jax.ShapeDtypeStruct((CHANNELS, count * 2, 128), jnp.float32),
             jax.ShapeDtypeStruct(geometry.shape, jnp.float32),
         ),
-        in_specs=[anywhere, anywhere],
+        in_specs=[in_vmem, in_vmem],
         out_specs=(anywhere, anywhere),
         scratch_shapes=[
-            pltpu.VMEM((count * 8, 128), jnp.int32),
-            pltpu.VMEM(geometry.shape, jnp.float32),
             pltpu.VMEM((CHANNELS, count * 2, 128), jnp.float32),
-            pltpu.SemaphoreType.DMA((2,)),
-            pltpu.SemaphoreType.DMA((pieces,)),
+            pltpu.SemaphoreType.DMA,
             pltpu.SemaphoreType.DMA((pieces,)),
         ],
-        compiler_params=pltpu.CompilerParams(vmem_limit_bytes=62 * 2**20),
+        compiler_params=pltpu.CompilerParams(vmem_limit_bytes=16 * 2**20),
     )(arrived.reshape(count * 8, 128), geometry)
     received = jnp.transpose(received, (1, 0, 2))[None]
     return (geometry.reshape(CHANNELS, 4, 8, 128), received)

time: 30.2 us -> 29.2 us (0.967)
  Pallas kernels: 29.4 us -> 28.4 us
    pallas_call x1, Pallas kernels: 1.97 us -> 1 us  [body(): pl.pallas_call(decode_kernel, out_shape=(jax.ShapeDtypeStruct((CHANNELS,...]
where the time goes in v5:
time: 29.2 us; the launch traced here: 29 us
  Pallas kernels  28.4 us (97%)
  between operations  0.64 us (2%)
    pallas_call x1, Pallas kernels, body(): pl.pallas_call(functools.partial(kernel, count_x, count_y), out_shape=(pl...  27.4 us
    pallas_call x1, Pallas kernels, body(): pl.pallas_call(decode_kernel, out_shape=(jax.ShapeDtypeStruct((CHANNELS,...  1 us

profile of v5, /device:TPU:1, one launch (start us, length us, event | category | flops | bytes accessed | tf_op | source)
XLA Modules:
  0.0 29.0 jit_solution(72851865495879059)
XLA Ops:
  0.6 27.4 %shard_map.140 = (f32[7,32,128]{2,1,0:T(8,128)S(1)}, s32[128,8,128]{2,1,0:T(8,128)S(1)}) custom-call(bf16[26,32,512]{2,1,0:T(8,128)(2,1)} %volume.1, s32[1,32]{1,0:T(1,128)} %bitcast.8, s32[1,32]{1,0:T(1,128)} %bitcast.9, f32[8,192]{1,0:T(8,128)} %constant.20.clone.marks_h, bf16[32,256]{1,0:T(8,128)(2,1)} %constant.21.clone.take_w, ...), custom_call_target="tpu_custom_call" | custom-call | tf_op jit(solution)/shard_map/pallas_call | solution.py:552
  28.0 1.0 %shard_map.141 = (f32[7,256,128]{2,1,0:T(8,128)}, f32[7,32,128]{2,1,0:T(8,128)}) custom-call(s32[1024,128]{1,0:T(8,128)S(1)} %bitcast.7, f32[7,32,128]{2,1,0:T(8,128)S(1)} %get-tuple-element.7.geometry_in), custom_call_target="tpu_custom_call" | custom-call | tf_op jit(solution)/shard_map/pallas_call | solution.py:596

commit v6 on v5

--- a/solution.py
+++ b/solution.py
@@ -206,7 +206,7 @@
     take_w, pack_w, own_w, main_w, put_w, inner_w, side_w, outer_w, cell_y_w,
     geometry_h, arrived,
     tile, packed, columns, corners, sides, beside, corner_in, ends, side_ends,
-    smooth, sharp, chosen, leaving, geometry, owner, flags, marks, main_v,
+    smooth, sharp, chosen, stacked, leaving, geometry, owner, flags, marks, main_v,
     take_v, pack_v, own_v, put_v, inner_v, side_v, outer_v, cell_y_v,
     load_sem, send_sem, recv_sem, far_sem, out_send, out_recv, own_sem, geometry_sem,
 ):
@@ -250,8 +250,12 @@
         ).astype(jnp.bfloat16)
 
     def put_columns(taken):
+        left_keep = jnp.where(q == 0, 0.0, 1.0)
+        right_keep = jnp.where(q == count_y - 1, 0.0, 1.0)
+        line = lax.broadcasted_iota(jnp.int32, (32, 128), 0)
+        inside = jnp.where(line < 16, left_keep, right_keep).astype(jnp.bfloat16)
         return lax.dot_general(
-            taken, put_v[...], (((0,), (0,)), ((), ())), preferred_element_type=jnp.float32
+            taken, put_v[...] * inside, (((0,), (0,)), ((), ())), preferred_element_type=jnp.float32
         ).astype(jnp.bfloat16)
 
     for load in loads[0:3]:
@@ -327,14 +331,6 @@
     for send in sends[0:2]:
         send.wait()
 
-    @pl.when(q == 0)
-    def _():
-        beside[0:16, :] = jnp.zeros((16, beside.shape[1]), jnp.bfloat16)
-
-    @pl.when(q == count_y - 1)
-    def _():
-        beside[16:32, :] = jnp.zeros((16, beside.shape[1]), jnp.bfloat16)
-
     lane = lax.broadcasted_iota(jnp.int32, (1, 128), 1)
     left_out = jnp.where(q == 0, 127, -1)
     right_out = jnp.where(q == count_y - 1, 0, -1)
@@ -392,28 +388,14 @@
     for send in sends[2:]:
         send.wait()
 
-    @pl.when(p == 0)
-    def _():
-        sides[0:SIDE_ROWS, :] = jnp.zeros((SIDE_ROWS, TILE_Y), jnp.bfloat16)
-        corner_in[0] = jnp.zeros(corner_in.shape[1:], jnp.bfloat16)
-
-    @pl.when(p == count_x - 1)
-    def _():
-        sides[SIDE_ROWS : 2 * SIDE_ROWS, :] = jnp.zeros((SIDE_ROWS, TILE_Y), jnp.bfloat16)
-        corner_in[1] = jnp.zeros(corner_in.shape[1:], jnp.bfloat16)
-
-    @pl.when(q == 0)
-    def _():
-        corner_in[:, 0:16, :] = jnp.zeros((2, 16, corner_in.shape[2]), jnp.bfloat16)
-
-    @pl.when(q == count_y - 1)
-    def _():
-        corner_in[:, 16:32, :] = jnp.zeros((2, 16, corner_in.shape[2]), jnp.bfloat16)
-
     for side in range(2):
         side_ends[side * SIDE_ROWS : (side + 1) * SIDE_ROWS, :] = put_columns(
             corner_in[side, :, 0:SIDE_ROWS]
         )
+    low_out = jnp.where(p == 0, 1.0, 0.0)
+    high_out = jnp.where(p == count_x - 1, 1.0, 0.0)
+    place = lax.broadcasted_iota(jnp.int32, (1, 2 * WINDOW), 1)
+    side_keep = jnp.where(place < WINDOW, 1.0 - low_out, 1.0 - high_out).astype(jnp.bfloat16)
     blurred = []
     for g in range(GROUPS):
         low_rows = slice(WINDOW_AT[g], WINDOW_AT[g] + WINDOW)
@@ -426,11 +408,11 @@
             axis=0,
         )
         blurred.append(
-            dot(side_v[g, 0], window) + dot(side_v[g, 1], window) + smooth[g, INNER:GROUP_ROWS, :]
+            dot(side_v[g, 0] * side_keep, window)
+            + dot(side_v[g, 1] * side_keep, window)
+            + smooth[g, INNER:GROUP_ROWS, :]
         )
     high, low = indicator(jnp.concatenate(blurred, axis=0))
-    low_out = jnp.where(p == 0, 1.0, 0.0)
-    high_out = jnp.where(p == count_x - 1, 1.0, 0.0)
     keep = (1.0 - low_out * marks[0:1, :] - high_out * marks[1:2, :]).astype(jnp.bfloat16)
     weights = outer_v[...] * keep
     cells = cells + dot(weights, high) + dot(weights, low)
@@ -464,26 +446,34 @@
         [jnp.concatenate(whole[0:4], axis=0), jnp.concatenate(whole[4:8], axis=0)], axis=1
     )
     upper = jnp.floor(coded * (1.0 / 256.0) + 0.5) * 256.0
-    stacked = jnp.concatenate([upper, coded - upper], axis=0).astype(jnp.bfloat16)
-    placed = dot(chosen[...], stacked).astype(jnp.int32)
-    joined = (placed[:, 128:256] << 16) | (placed[:, 0:128] & 0xFFFF)
-    leaving[...] = joined.reshape(count, 8, 128)
-
+    stacked[...] = jnp.concatenate([upper, coded - upper], axis=0).astype(jnp.bfloat16)
+
+    def send_to_row(offset, first_step):
+        other_p = lax.rem(p + offset, count_x)
+        rows = pl.ds(pl.multiple_of(other_p * (count_y * 8), count_y * 8), count_y * 8)
+        placed = dot(chosen[rows, :], stacked[...]).astype(jnp.int32)
+        joined = (placed[:, 128:256] << 16) | (placed[:, 0:128] & 0xFFFF)
+        leaving[pl.ds(other_p * count_y, count_y)] = joined.reshape(count_y, 8, 128)
+        for step in range(first_step, count_y):
+            other_q = lax.rem(q + step, count_y)
+            pltpu.make_async_remote_copy(
+                src_ref=leaving.at[other_p * count_y + other_q],
+                dst_ref=arrived.at[me],
+                send_sem=out_send,
+                recv_sem=out_recv,
+                device_id=(other_p, other_q),
+                device_id_type=MESH,
+            ).start()
+
+    def send_rows(offset, carry):
+        send_to_row(offset, 0)
+        return carry
+
+    send_to_row(0, 1)
+    lax.fori_loop(1, 5, send_rows, 0)
+    lax.fori_loop(count_x - 4, count_x, send_rows, 0)
     pl.semaphore_wait(far_sem.at[2], 2)
-
-    def send_out(step, carry):
-        other = lax.rem(me + step, count)
-        pltpu.make_async_remote_copy(
-            src_ref=leaving.at[other],
-            dst_ref=arrived.at[me],
-            send_sem=out_send,
-            recv_sem=out_recv,
-            device_id=(other // count_y, lax.rem(other, count_y)),
-            device_id_type=MESH,
-        ).start()
-        return carry
-
-    lax.fori_loop(1, count, send_out, 0)
+    lax.fori_loop(5, count_x - 4, send_rows, 0)
     stay = pltpu.make_async_copy(leaving.at[me], arrived.at[me], own_sem)
     stay.start()
     others = pl.ds(0, count - 1)
@@ -570,6 +560,7 @@
             pltpu.VMEM((GROUPS, GROUP_ROWS, WIDE_Y), jnp.float32),
             pltpu.VMEM((2, GROUPS * INNER, WIDE_Y), bf16),
             pltpu.VMEM((count * 8, 256), bf16),
+            pltpu.VMEM((256, 256), bf16),
             pltpu.VMEM((count, 8, 128), jnp.int32),
             pltpu.VMEM((CHANNELS, ROWS, 128), jnp.float32),
             pltpu.VMEM((1, ROWS), jnp.int32),

time: 29.2 us -> 29 us (level)
  no operation moved by 1% of the time
where the time goes in v6:
time: 29 us; the launch traced here: 28.9 us
  Pallas kernels  28.2 us (97%)
  between operations  0.64 us (2%)
    pallas_call x1, Pallas kernels, body(): pl.pallas_call(functools.partial(kernel, count_x, count_y), out_shape=(pl...  27.2 us
    pallas_call x1, Pallas kernels, body(): pl.pallas_call(decode_kernel, out_shape=(jax.ShapeDtypeStruct((CHANNELS,...  1 us

profile of v6, /device:TPU:1, one launch (start us, length us, event | category | flops | bytes accessed | tf_op | source)
XLA Modules:
  0.0 28.9 jit_solution(17908881612002352509)
XLA Ops:
  0.6 27.2 %shard_map.140 = (f32[7,32,128]{2,1,0:T(8,128)S(1)}, s32[128,8,128]{2,1,0:T(8,128)S(1)}) custom-call(bf16[26,32,512]{2,1,0:T(8,128)(2,1)} %volume.1, s32[1,32]{1,0:T(1,128)} %bitcast.8, s32[1,32]{1,0:T(1,128)} %bitcast.9, f32[8,192]{1,0:T(8,128)} %constant.20.clone.marks_h, bf16[32,256]{1,0:T(8,128)(2,1)} %constant.21.clone.take_w, ...), custom_call_target="tpu_custom_call" | custom-call | tf_op jit(solution)/shard_map/pallas_call | solution.py:542
  27.9 1.0 %shard_map.141 = (f32[7,256,128]{2,1,0:T(8,128)}, f32[7,32,128]{2,1,0:T(8,128)}) custom-call(s32[1024,128]{1,0:T(8,128)S(1)} %bitcast.7, f32[7,32,128]{2,1,0:T(8,128)S(1)} %get-tuple-element.7.geometry_in), custom_call_target="tpu_custom_call" | custom-call | tf_op jit(solution)/shard_map/pallas_call | solution.py:587

commit v7 on v6

--- a/solution.py
+++ b/solution.py
@@ -279,9 +279,6 @@
         )
 
     pl.semaphore_wait(barrier, len(around))
-    diagonals = around[4:]
-    for dx, dy in diagonals:
-        pl.semaphore_signal(far_sem.at[0], inc=1, device_id=at(dx, dy), device_id_type=MESH)
     sends = []
     for i, (dx, dy) in enumerate(around):
         rows, rows_there = (0, SIDE_ROWS) if dx < 0 else (SIDE_ROWS, 0)
@@ -307,6 +304,9 @@
         )
     for send in sends:
         send.start()
+    diagonals = around[4:]
+    for dx, dy in diagonals:
+        pl.semaphore_signal(far_sem.at[0], inc=1, device_id=at(dx, dy), device_id_type=MESH)
 
     loads[3].wait()
     for g in range(GROUPS):

time: 29 us -> 29 us (level)
  no operation moved by 1% of the time
where the time goes in v7:
time: 29 us; the launch traced here: 28.9 us
  Pallas kernels  28.2 us (97%)
  between operations  0.64 us (2%)
    pallas_call x1, Pallas kernels, body(): pl.pallas_call(functools.partial(kernel, count_x, count_y), out_shape=(pl...  27.2 us
    pallas_call x1, Pallas kernels, body(): pl.pallas_call(decode_kernel, out_shape=(jax.ShapeDtypeStruct((CHANNELS,...  1 us

profile of v7, /device:TPU:1, one launch (start us, length us, event | category | flops | bytes accessed | tf_op | source)
XLA Modules:
  0.0 28.9 jit_solution(6733168428760618398)
XLA Ops:
  0.6 27.2 %shard_map.140 = (f32[7,32,128]{2,1,0:T(8,128)S(1)}, s32[128,8,128]{2,1,0:T(8,128)S(1)}) custom-call(bf16[26,32,512]{2,1,0:T(8,128)(2,1)} %volume.1, s32[1,32]{1,0:T(1,128)} %bitcast.8, s32[1,32]{1,0:T(1,128)} %bitcast.9, f32[8,192]{1,0:T(8,128)} %constant.20.clone.marks_h, bf16[32,256]{1,0:T(8,128)(2,1)} %constant.21.clone.take_w, ...), custom_call_target="tpu_custom_call" | custom-call | tf_op jit(solution)/shard_map/pallas_call | solution.py:542
  27.9 1.0 %shard_map.141 = (f32[7,256,128]{2,1,0:T(8,128)}, f32[7,32,128]{2,1,0:T(8,128)}) custom-call(s32[1024,128]{1,0:T(8,128)S(1)} %bitcast.7, f32[7,32,128]{2,1,0:T(8,128)S(1)} %get-tuple-element.7.geometry_in), custom_call_target="tpu_custom_call" | custom-call | tf_op jit(solution)/shard_map/pallas_call | solution.py:587

commit v8 on v7

--- a/solution.py
+++ b/solution.py
@@ -220,8 +220,6 @@
 
     around = [(0, -1), (0, 1), (-1, 0), (1, 0), (-1, -1), (-1, 1), (1, -1), (1, 1)]
     barrier = pltpu.get_barrier_semaphore()
-    for dx, dy in around:
-        pl.semaphore_signal(barrier, inc=1, device_id=at(dx, dy), device_id_type=MESH)
     pairs = [
         (volume, tile),
         (pack_w, pack_v),
@@ -238,7 +236,10 @@
         (cell_y_w, cell_y_v),
     ]
     loads = [pltpu.make_async_copy(*pair, load_sem.at[i]) for i, pair in enumerate(pairs)]
-    for load in loads[0:4]:
+    loads[0].start()
+    for dx, dy in around:
+        pl.semaphore_signal(barrier, inc=1, device_id=at(dx, dy), device_id_type=MESH)
+    for load in loads[1:4]:
         load.start()
     main_v[:, 0 : BAND[0], :] = jnp.zeros((2, BAND[0], 256), jnp.bfloat16)
     main_v[:, BAND[1] : 512, :] = jnp.zeros((2, 512 - BAND[1], 256), jnp.bfloat16)

time: 29 us -> 28.9 us (level)
  no operation moved by 1% of the time
where the time goes in v8:
time: 28.9 us; the launch traced here: 28.8 us
  Pallas kernels  28.1 us (97%)
  between operations  0.64 us (2%)
    pallas_call x1, Pallas kernels, body(): pl.pallas_call(functools.partial(kernel, count_x, count_y), out_shape=(pl...  27.1 us
    pallas_call x1, Pallas kernels, body(): pl.pallas_call(decode_kernel, out_shape=(jax.ShapeDtypeStruct((CHANNELS,...  1 us

profile of v8, /device:TPU:1, one launch (start us, length us, event | category | flops | bytes accessed | tf_op | source)
XLA Modules:
  0.0 28.8 jit_solution(1560029753919489457)
XLA Ops:
  0.6 27.1 %shard_map.140 = (f32[7,32,128]{2,1,0:T(8,128)S(1)}, s32[128,8,128]{2,1,0:T(8,128)S(1)}) custom-call(bf16[26,32,512]{2,1,0:T(8,128)(2,1)} %volume.1, s32[1,32]{1,0:T(1,128)} %bitcast.8, s32[1,32]{1,0:T(1,128)} %bitcast.9, f32[8,192]{1,0:T(8,128)} %constant.20.clone.marks_h, bf16[32,256]{1,0:T(8,128)(2,1)} %constant.21.clone.take_w, ...), custom_call_target="tpu_custom_call" | custom-call | tf_op jit(solution)/shard_map/pallas_call | solution.py:543
  27.8 1.0 %shard_map.141 = (f32[7,256,128]{2,1,0:T(8,128)}, f32[7,32,128]{2,1,0:T(8,128)}) custom-call(s32[1024,128]{1,0:T(8,128)S(1)} %bitcast.7, f32[7,32,128]{2,1,0:T(8,128)S(1)} %get-tuple-element.7.geometry_in), custom_call_target="tpu_custom_call" | custom-call | tf_op jit(solution)/shard_map/pallas_call | solution.py:588
